TPU v7x, 128 devices: a whole 4x4x4 slice. The times are simulated.
128 devices in a mesh: dp: 32 (over x, z, core), sub: 4 (over y).
Axes of the slice: x: 4, y: 4, z: 4, core: 2. Of those that a mesh axis runs over, the one named last changes fastest.
Arguments:
- vector_window: bfloat16 [131072, 1024], P(('dp', 'sub')), may hold values from -6 to 6
- orthogonal_matrix: bfloat16 [1024, 1024], replicated, may hold values from -0.1875 to 0.1875
- centroid_table: bfloat16 [4, 2048, 256], P('sub', 'dp'), may hold values from -3.4 to 3.4
- sharpness_scale: float32 [4], replicated, may hold values from 0.25 to 1
Outputs:
- new_codebook: float32 [4, 2048, 256], P('sub', 'dp')
- recon: bfloat16 [131072, 1024], P(('dp', 'sub'))
- cross_cov: float32 [1024, 1024], replicated
All inputs are finite; a program needn't handle non-finite values.
Results may differ from a plain program's by a relative error of at most 0.014.
Values may be sent and summed in bfloat16 or wider, within the bound.
A program may use at most 128 MiB of HBM per device.

v0:
```python
import math

import jax
import jax.numpy as jnp
from jax import lax
from jax.sharding import PartitionSpec as P


def allot_part_vectors(sample_vectors, centroid_entry, sharpness_factor):
    count_rows = sample_vectors.shape[0]
    width = sample_vectors.shape[1]
    words = centroid_entry.shape[0]
    block = min(1024, count_rows)
    blocks = sample_vectors.reshape(count_rows // block, block, width)
    centroid_norm_squared = jnp.sum(centroid_entry.astype(jnp.float32) ** 2, axis=1)

    def step(carry, block_index):
        centroid_totals, centroid_tallies = carry
        raw_scores = sharpness_factor * (
            2.0 * jnp.dot(block_index, centroid_entry.T, preferred_element_type=jnp.float32)
            - centroid_norm_squared[None, :]
        )
        probs = jax.nn.softmax(raw_scores, axis=1).astype(jnp.bfloat16)
        restored_vectors = jnp.dot(
            probs, centroid_entry, preferred_element_type=jnp.float32
        ).astype(jnp.bfloat16)
        centroid_totals = centroid_totals + lax.dot_general(
            probs, block_index, (((0,), (0,)), ((), ())), preferred_element_type=jnp.float32
        )
        centroid_tallies = centroid_tallies + jnp.sum(probs.astype(jnp.float32), axis=0)
        return ((centroid_totals, centroid_tallies), restored_vectors)

    init = (jnp.zeros((words, width), jnp.float32), jnp.zeros((words,), jnp.float32))
    (centroid_totals, centroid_tallies), restored_vectors = lax.scan(step, init, blocks)
    return (restored_vectors.reshape(count_rows, width), centroid_totals, centroid_tallies)


def body(vector_window, orthogonal_matrix, centroid_table, sharpness_scale):
    turned_vectors = jnp.dot(
        vector_window, orthogonal_matrix, preferred_element_type=jnp.float32
    ).astype(jnp.bfloat16)
    entire_vocabulary = lax.all_gather(centroid_table, "dp", axis=1, tiled=True)
    member_vectors = lax.all_to_all(turned_vectors, "sub", split_axis=1, concat_axis=0, tiled=True)
    sharpness_factor = lax.dynamic_slice_in_dim(sharpness_scale, lax.axis_index("sub"), 1)[0]
    restored_vectors, centroid_totals, centroid_tallies = allot_part_vectors(
        member_vectors, entire_vocabulary[0], sharpness_factor
    )
    recon = lax.all_to_all(restored_vectors, "sub", split_axis=0, concat_axis=1, tiled=True)
    group_sums = centroid_totals[None]
    group_counts = centroid_tallies[None]
    owned_sums, owned_counts = (
        lax.psum_scatter(
            group_sums.astype(jnp.bfloat16), "dp", scatter_dimension=1, tiled=True
        ).astype(jnp.float32),
        lax.psum_scatter(
            group_counts.astype(jnp.bfloat16), "dp", scatter_dimension=1, tiled=True
        ).astype(jnp.float32),
    )
    new_codebook = (owned_sums + centroid_table.astype(jnp.float32)) / (
        owned_counts[:, :, None] + 1.0
    )
    partial_value = lax.dot_general(
        vector_window, recon, (((0,), (0,)), ((), ())), preferred_element_type=jnp.float32
    )
    total_rows = vector_window.shape[0] * lax.axis_size("dp") * lax.axis_size("sub")
    cross_cov = lax.psum(partial_value, ("dp", "sub")) / math.sqrt(total_rows)
    return (new_codebook, recon, cross_cov)


def solution(mesh):
    placed = (P(("dp", "sub"), None), P(), P("sub", "dp", None), P())
    return jax.shard_map(
        body,
        mesh=mesh,
        in_specs=placed,
        out_specs=(P("sub", "dp", None), P(("dp", "sub"), None), P()),
        check_vma=False,
    )
```

profile of v0, /device:TPU:1, one launch (start us, length us, event | category | flops | bytes accessed | tf_op | source)
XLA Modules:
  0.0 476.1 jit_solution(9173983727400559610)
XLA Ops:
  7.2 0.0 copy-start
  7.2 0.0 all-gather.2.cloned.1.call-start
  7.2 0.7 all-gather.2.cloned.1.call-update
  7.9 0.8 copy-done
  8.8 5.3 %convolution_convert_fusion.1 = bf16[1024,1024]{0,1:T(8,128)(2,1)} fusion(bf16[1024,1024]{1,0:T(8,128)(2,1)S(1)} %copy-done, bf16[1024,1024]{1,0:T(8,128)(2,1)} %param.7), kind=kOutput, calls=%fused_computation.21 | convolution fusion | flops 2148532224 | bytes 6291456 | tf_op jit(solution)/shard_map/dot_general | solution.py:39
  14.1 3.9 copy.10
  18.0 5.0 %all-to-all-start = ((bf16[1024,4,256]{2,0,1:T(8,128)(2,1)}), bf16[1024,4,256]{2,0,1:T(8,128)(2,1)}, u32[]{:S(2)}, u32[]{:S(2)}) async-start(bf16[1024,4,256]{2,0,1:T(8,128)(2,1)} %copy.10), calls=%async_computation | async-start | bytes 4194304 | tf_op jit(solution)/shard_map/all_to_all | solution.py:43
  23.0 0.0 copy-done.5
  23.0 0.6 dynamic_slice.7
  23.6 33.2 %all-gather.2.cloned.1.call-done = bf16[1,2048,256]{2,1,0:T(8,128)(2,1)} async-done(((bf16[1,64,256]{2,1,0:T(8,128)(2,1)}), bf16[1,2048,256]{2,1,0:T(8,128)(2,1)}) %all-gather.2.cloned.1.call-update) | async-done | bytes 1048592 | tf_op jit(solution)/shard_map/all_gather | solution.py:42
  56.8 1.6 multiply_reduce_fusion
  58.4 0.0 all-to-all-done
  58.4 75.6 %while.15 = (s32[]{:T(128)}, f32[2048,256]{1,0:T(8,128)}, f32[2048]{0:T(1024)S(1)}, bf16[4,1024,256]{2,1,0:T(8,128)(2,1)}, f32[]{:T(128)}, /*index=5*/bf16[4,102...) while((s32[]{:T(128)}, f32[2048,256]{1,0:T(8,128)}, ...), condition=%wide.region_5.6_spmd.clone, body=%wide.region_1.5_spmd.clone.sunk | while | flops 3258187776 | bytes 66664620 | solution.py:34
  58.4 3.4 fusion.32
  61.9 3.1 fusion.33
  65.0 4.6 convert_reduce_fusion.2
  69.6 5.1 %convolution_add_fusion.2 = f32[2048,256]{1,0:T(8,128)} fusion(bf16[1024,2048]{1,0:T(8,128)(2,1)} %get-tuple-element.158, f32[2048,256]{1,0:T(8,128)} %get-tuple-element.171, pred[]{:T(512)S(6)} %compare.3, bf16[4,1024,256]{2,1,0:T(8,128)(2,1)} %get-tuple-element.185, s32[]{:T(128)} %get-tuple-element.170), kind=kOutput, calls=%fused_computation.6.clone.1 | convolution fusion | flops 1074790400 | bytes 8913409 | tf_op jit(solution)/shard_map/while/body/eval_jaxpr/dot_general | solution.py:27
  74.7 0.0 copy-done.1
  74.7 0.0 copy-done.3
  74.7 2.1 fusion.34
  76.8 3.4 fusion.32
  80.2 3.1 fusion.33
  83.3 4.6 convert_reduce_fusion.2
  88.0 5.8 %convolution_add_fusion.2 = f32[2048,256]{1,0:T(8,128)} fusion(bf16[1024,2048]{1,0:T(8,128)(2,1)} %get-tuple-element.158, f32[2048,256]{1,0:T(8,128)} %get-tuple-element.171, pred[]{:T(512)S(6)} %compare.3, bf16[4,1024,256]{2,1,0:T(8,128)(2,1)} %get-tuple-element.185, s32[]{:T(128)} %get-tuple-element.170), kind=kOutput, calls=%fused_computation.6.clone.1 | convolution fusion | flops 1074790400 | bytes 8913409 | tf_op jit(solution)/shard_map/while/body/eval_jaxpr/dot_general | solution.py:27
  93.8 0.0 copy-done.1
  93.8 0.0 copy-done.3
  93.8 2.1 fusion.34
  95.9 3.4 fusion.32
  99.3 3.1 fusion.33
  102.4 4.6 convert_reduce_fusion.2
  107.0 5.8 %convolution_add_fusion.2 = f32[2048,256]{1,0:T(8,128)} fusion(bf16[1024,2048]{1,0:T(8,128)(2,1)} %get-tuple-element.158, f32[2048,256]{1,0:T(8,128)} %get-tuple-element.171, pred[]{:T(512)S(6)} %compare.3, bf16[4,1024,256]{2,1,0:T(8,128)(2,1)} %get-tuple-element.185, s32[]{:T(128)} %get-tuple-element.170), kind=kOutput, calls=%fused_computation.6.clone.1 | convolution fusion | flops 1074790400 | bytes 8913409 | tf_op jit(solution)/shard_map/while/body/eval_jaxpr/dot_general | solution.py:27
  112.9 0.0 copy-done.1
  112.9 0.0 copy-done.3
  112.9 2.0 fusion.34
  114.9 3.4 fusion.32
  118.3 3.1 fusion.33
  121.4 4.6 convert_reduce_fusion.2
  126.1 5.8 %convolution_add_fusion.2 = f32[2048,256]{1,0:T(8,128)} fusion(bf16[1024,2048]{1,0:T(8,128)(2,1)} %get-tuple-element.158, f32[2048,256]{1,0:T(8,128)} %get-tuple-element.171, pred[]{:T(512)S(6)} %compare.3, bf16[4,1024,256]{2,1,0:T(8,128)(2,1)} %get-tuple-element.185, s32[]{:T(128)} %get-tuple-element.170), kind=kOutput, calls=%fused_computation.6.clone.1 | convolution fusion | flops 1074790400 | bytes 8913409 | tf_op jit(solution)/shard_map/while/body/eval_jaxpr/dot_general | solution.py:27
  131.9 0.0 copy-done.1
  131.9 0.0 copy-done.3
  131.9 2.1 fusion.34
  134.0 4.4 all-to-all-start.1
  138.4 0.0 reduce-scatter.7.cloned.1.call-start
  138.5 1.2 reshape_bitcast_fusion
  139.6 0.0 reduce-scatter.7.cloned.1.call-update
  139.7 0.0 reduce-scatter.5.cloned.1.call-start
  139.7 2.7 convert_bitcast_fusion
  142.4 0.0 reduce-scatter.5.cloned.1.call-update
  142.4 0.2 all-reduce.2.cloned.1.call-start
  142.6 22.1 %all-to-all-done.1 = bf16[4,1024,256]{2,1,0:T(8,128)(2,1)} async-done(((bf16[4,1024,256]{2,1,0:T(8,128)(2,1)}), bf16[4,1024,256]{2,1,0:T(8,128)(2,1)}, u32[]{:S(2)}, u32[]{:S(2)}) %all-to-all-start.1) | async-done | bytes 2097184 | tf_op jit(solution)/shard_map/all_to_all | solution.py:48
  164.7 1.9 copy.15
  166.6 0.0 copy-start.2
  166.6 1.3 copy-done.2
  168.0 4.4 convolution_bitcast_fusion
  172.4 0.0 all-reduce.2.cloned.1.call-update
  172.4 45.1 %reduce-scatter.7.cloned.1.call-done = bf16[64,1]{1,0:T(8,128)(2,1)} async-done(((bf16[2048,1]{1,0:T(8,128)(2,1)}), bf16[64,1]{1,0:T(8,128)(2,1)}) %reduce-scatter.7.cloned.1.call-update) | async-done | bytes 144
  217.5 0.7 add_bitcast_fusion
  218.3 0.1 copy.16
  218.3 79.6 %reduce-scatter.5.cloned.1.call-done = bf16[1,64,256]{2,1,0:T(8,128)(2,1)} async-done(((bf16[1,2048,256]{2,1,0:T(8,128)(2,1)}), bf16[1,64,256]{2,1,0:T(8,128)(2,1)}) %reduce-scatter.5.cloned.1.call-update) | async-done | bytes 32784 | tf_op jit(solution)/shard_map/reduce_scatter | solution.py:52
  298.0 0.0 copy-done.4
  298.0 1.5 add_divide_fusion
  299.4 159.7 %all-reduce.2.cloned.1.call-done = f32[1024,1024]{0,1:T(8,128)} async-done(((f32[1024,1024]{0,1:T(8,128)}), f32[1024,1024]{0,1:T(8,128)}) %all-reduce.2.cloned.1.call-update) | async-done | bytes 4194320 | tf_op jit(solution)/shard_map/psum | solution.py:66
  459.1 5.1 %broadcast_multiply_fusion = f32[1024,1024]{0,1:T(8,128)} fusion(f32[1024,1024]{0,1:T(8,128)} %all-reduce.2.cloned.1.call-done), kind=kLoop, calls=%fused_computation.19 | loop fusion | flops 1048576 | bytes 8388608 | tf_op jit(solution)/shard_map/div | solution.py:66
  464.2 5.3 %copy.12 = f32[1024,1024]{1,0:T(8,128)} copy(f32[1024,1024]{0,1:T(8,128)} %broadcast_multiply_fusion) | data formatting | bytes 8388608
  (18 shorter events, 0.0 us)
Async XLA Ops:
  7.2 1.6 copy-start
  7.2 49.6 %all-gather.2.cloned.1.call-start = ((), (), s32[]{:S(2)}) async-start(), calls=%async_computation.4 | async-start | bytes 1081344 | tf_op jit(solution)/shard_map/all_gather | solution.py:42
  14.1 9.0 %copy-start.5 = (f32[4]{0:T(128)S(1)}, f32[4]{0:T(128)}, u32[]{:S(2)}) copy-start(f32[4]{0:T(128)} %param.9) | copy-start | bytes 52
  18.0 40.4 %all-to-all-start = ((bf16[1024,4,256]{2,0,1:T(8,128)(2,1)}), bf16[1024,4,256]{2,0,1:T(8,128)(2,1)}, u32[]{:S(2)}, u32[]{:S(2)}) async-start(bf16[1024,4,256]{2,0,1:T(8,128)(2,1)} %copy.10), calls=%async_computation | async-start | bytes 4194304 | tf_op jit(solution)/shard_map/all_to_all | solution.py:43
  69.6 5.1 %copy-start.1 = (bf16[1024,2048]{1,0:T(8,128)(2,1)S(1)}, bf16[1024,2048]{1,0:T(8,128)(2,1)}, u32[]{:S(2)}) copy-start(bf16[1024,2048]{1,0:T(8,128)(2,1)} %get-tuple-element.158) | copy-start | bytes 12582916 | tf_op jit(solution)/shard_map/while
  69.6 5.1 %copy-start.3 = (bf16[2048,256]{1,0:T(8,128)(2,1)S(1)}, bf16[2048,256]{1,0:T(8,128)(2,1)}, u32[]{:S(2)}) copy-start(bf16[2048,256]{1,0:T(8,128)(2,1)} %get-tuple-element.186) | copy-start | bytes 3145732 | tf_op jit(solution)/shard_map/while
  87.9 5.8 %copy-start.1 = (bf16[1024,2048]{1,0:T(8,128)(2,1)S(1)}, bf16[1024,2048]{1,0:T(8,128)(2,1)}, u32[]{:S(2)}) copy-start(bf16[1024,2048]{1,0:T(8,128)(2,1)} %get-tuple-element.158) | copy-start | bytes 12582916 | tf_op jit(solution)/shard_map/while
  87.9 5.8 %copy-start.3 = (bf16[2048,256]{1,0:T(8,128)(2,1)S(1)}, bf16[2048,256]{1,0:T(8,128)(2,1)}, u32[]{:S(2)}) copy-start(bf16[2048,256]{1,0:T(8,128)(2,1)} %get-tuple-element.186) | copy-start | bytes 3145732 | tf_op jit(solution)/shard_map/while
  107.0 5.8 %copy-start.1 = (bf16[1024,2048]{1,0:T(8,128)(2,1)S(1)}, bf16[1024,2048]{1,0:T(8,128)(2,1)}, u32[]{:S(2)}) copy-start(bf16[1024,2048]{1,0:T(8,128)(2,1)} %get-tuple-element.158) | copy-start | bytes 12582916 | tf_op jit(solution)/shard_map/while
  107.0 5.8 %copy-start.3 = (bf16[2048,256]{1,0:T(8,128)(2,1)S(1)}, bf16[2048,256]{1,0:T(8,128)(2,1)}, u32[]{:S(2)}) copy-start(bf16[2048,256]{1,0:T(8,128)(2,1)} %get-tuple-element.186) | copy-start | bytes 3145732 | tf_op jit(solution)/shard_map/while
  126.1 5.8 %copy-start.1 = (bf16[1024,2048]{1,0:T(8,128)(2,1)S(1)}, bf16[1024,2048]{1,0:T(8,128)(2,1)}, u32[]{:S(2)}) copy-start(bf16[1024,2048]{1,0:T(8,128)(2,1)} %get-tuple-element.158) | copy-start | bytes 12582916 | tf_op jit(solution)/shard_map/while
  126.1 5.8 %copy-start.3 = (bf16[2048,256]{1,0:T(8,128)(2,1)S(1)}, bf16[2048,256]{1,0:T(8,128)(2,1)}, u32[]{:S(2)}) copy-start(bf16[2048,256]{1,0:T(8,128)(2,1)} %get-tuple-element.186) | copy-start | bytes 3145732 | tf_op jit(solution)/shard_map/while
  134.0 30.8 %all-to-all-start.1 = ((bf16[4,1024,256]{2,1,0:T(8,128)(2,1)}), bf16[4,1024,256]{2,1,0:T(8,128)(2,1)}, u32[]{:S(2)}, u32[]{:S(2)}) async-start(bf16[4,1024,256]{2,1,0:T(8,128)(2,1)} %get-tuple-element.49), calls=%async_computation.2 | async-start | bytes 4194304 | tf_op jit(solution)/shard_map/all_to_all | solution.py:48
  138.4 79.1 %reduce-scatter.7.cloned.1.call-start = ((), (), s32[]{:S(2)}) async-start(), calls=%async_computation.7 | async-start | bytes 540672
  139.7 158.3 %reduce-scatter.5.cloned.1.call-start = ((), (), s32[]{:S(2)}) async-start(), calls=%async_computation.5 | async-start | bytes 1081344 | tf_op jit(solution)/shard_map/reduce_scatter | solution.py:52
  142.4 316.7 %all-reduce.2.cloned.1.call-start = ((), (), s32[]{:S(2)}) async-start(), calls=%async_computation.6 | async-start | bytes 8388608 | tf_op jit(solution)/shard_map/psum | solution.py:66
  166.6 1.3 copy-start.2
  172.4 125.6 %copy-start.4 = (bf16[1,64,256]{2,1,0:T(8,128)(2,1)S(1)}, bf16[1,64,256]{2,1,0:T(8,128)(2,1)}, u32[]{:S(2)}) copy-start(bf16[1,64,256]{2,1,0:T(8,128)(2,1)} %param.8) | copy-start | bytes 98308
Sparse Core Ops, SparseCore 0:
  10.3 46.5 all-gather.1
  142.7 74.7 reduce-scatter.6
  221.0 76.8 reduce-scatter.4
  304.1 154.9 all-reduce.1
where the time goes:
time: 477 us; the launch traced here: 476 us
  waiting for transfers between devices  340 us (71%)
  matrix products  54.3 us (11%)
  other arithmetic  42.4 us (9%)
  local copies, waits for them, and re-layouts  15.2 us (3%)
  between operations  13.8 us (3%)
  starting transfers between devices  9.8 us (2%)
    psum x1, waiting for transfers between devices, body(): cross_cov = lax.psum(partial_value, ('dp', 'sub')) / math.sqrt(total_rows)  160 us
    reduce_scatter x1, waiting for transfers between devices, body(): lax.psum_scatter(group_sums.astype(jnp.bfloat16), 'dp', scatter_dimension...  79.6 us
    unnamed x5, waiting for transfers between devices  45.9 us
    all_gather x1, waiting for transfers between devices, body(): entire_vocabulary = lax.all_gather(centroid_table, 'dp', axis=1, tiled=True)  33.2 us
    dot_general x4, matrix products, step(): lax.dot_general(probs, block_index, (((0,), (0,)), ((), ())), preferred_e...  22.6 us
    all_to_all x1, waiting for transfers between devices, body(): lax.all_to_all(restored_vectors, 'sub', split_axis=0, concat_axis=1, tile...  22.1 us
    reduce_sum x4, other arithmetic, step(): jnp.sum(probs.astype(jnp.float32), axis=0)  18.5 us
    dot_general x4, matrix products, step(): jnp.dot(block_index, centroid_entry.T, preferred_element_type=jnp.float32)  13.7 us
  transfers between devices with their start and end apart: 6, of which 5 were waited for; matrix products, arithmetic and copies ran while one was open for 5% of the time, Pallas kernels for 0%

commit v1 on v0

v1 whole, which is shorter than its diff:
```python
import math

import jax
import jax.numpy as jnp
from jax import lax
from jax.experimental import pallas as pl
from jax.experimental.pallas import tpu as pltpu
from jax.sharding import PartitionSpec as P

LOG2E = math.log2(math.e)
G, F, K, D, R = 4, 256, 2048, 1024, 1024
RB = 256
NB = R // RB
KC = 256
NK = K // KC
f32, bf16 = jnp.float32, jnp.bfloat16
MESH = pl.DeviceIdType.MESH
VM = pl.BlockSpec(memory_space=pltpu.VMEM)


def dot(a, b):
    return jnp.dot(a, b, preferred_element_type=f32)


class Place:
    def __init__(self):
        dp, self.y = lax.axis_index("dp"), lax.axis_index("sub")
        self.x, self.z, self.c = dp // 8, (dp // 2) % 4, dp % 2

    def at(self, axis):
        return {"x": self.x, "y": self.y, "z": self.z}[axis]

    def step(self, axis, d):
        return (self.at(axis) + d) % 4

    def peer(self, axis, d):
        x, y, z = self.x, self.y, self.z
        if axis == "x":
            x = self.step("x", d)
        if axis == "y":
            y = self.step("y", d)
        if axis == "z":
            z = self.step("z", d)
        return ((x * 4 + z) * 2 + self.c, y)

    def sibling(self):
        return ((self.x * 4 + self.z) * 2 + 1 - self.c, self.y)

    def greet(self):
        barrier = pltpu.get_barrier_semaphore()
        for axis in "xyz":
            for d in (1, 2, 3):
                pl.semaphore_signal(barrier, inc=1, device_id=self.peer(axis, d), device_id_type=MESH)
        pl.semaphore_signal(barrier, inc=1, device_id=self.sibling(), device_id_type=MESH)
        pl.semaphore_wait(barrier, 10)


class Sems:
    def __init__(self, send, recv):
        self.send, self.recv, self.n = send, recv, 0

    def copy(self, src, dst, device):
        i = self.n
        self.n += 1
        op = pltpu.make_async_remote_copy(
            src_ref=src, dst_ref=dst, send_sem=self.send.at[i], recv_sem=self.recv.at[i],
            device_id=device, device_id_type=MESH,
        )
        op.start()
        return op


def wait(copies):
    for op in copies:
        op.wait()


GATHER_COPIES = 3 + G * 13


def gather_kernel(own_ref, cb_ref, send, recv, local):
    me = Place()
    sems = Sems(send, recv)
    x, y, z, c = me.x, me.y, me.z, me.c
    mine = pltpu.make_async_copy(own_ref.at[0], cb_ref.at[y, x, z, c], local)
    mine.start()
    me.greet()
    ops = [sems.copy(own_ref.at[0], cb_ref.at[y, x, z, c], me.peer("y", d)) for d in (1, 2, 3)]
    mine.wait()
    wait(ops)
    top, low = pl.ds(0, 32), pl.ds(32, 32)
    first = []
    for g in range(G):
        a, b = cb_ref.at[g, x, z, c, top], cb_ref.at[g, x, z, c, low]
        first.append(
            [sems.copy(a, a, me.peer("x", d)) for d in (1, 2, 3)]
            + [sems.copy(b, b, me.peer("z", d)) for d in (1, 2, 3)]
        )
    second = []
    for g in range(G):
        wait(first[g])
        a, b = cb_ref.at[g, :, z, c, top], cb_ref.at[g, x, :, c, low]
        second.append(
            [sems.copy(a, a, me.peer("z", d)) for d in (1, 2, 3)]
            + [sems.copy(b, b, me.peer("x", d)) for d in (1, 2, 3)]
        )
    last = []
    for g in range(G):
        wait(second[g])
        a = cb_ref.at[g, :, :, c]
        last.append(sems.copy(a, a, me.sibling()))
    wait(last)


def gather(own):
    return pl.pallas_call(
        gather_kernel,
        out_shape=jax.ShapeDtypeStruct((G, 4, 4, 2, 64, F), bf16),
        in_specs=[VM],
        out_specs=VM,
        scratch_shapes=[
            pltpu.SemaphoreType.DMA((GATHER_COPIES,)),
            pltpu.SemaphoreType.DMA((GATHER_COPIES,)),
            pltpu.SemaphoreType.DMA,
        ],
        compiler_params=pltpu.CompilerParams(collective_id=0, has_side_effects=True, vmem_limit_bytes=48 << 20),
        name="gather_codewords",
    )(own)


def compute_kernel(s_ref, x_ref, rot_ref, cb_ref, recon_ref, sums_ref, cnt_ref, cross_ref,
                   y_ref, yt_ref, xt_ref, ct_ref, b_ref, l0, l1, p0, p1):
    for g in range(G):
        cols = pl.ds(g * F, F)

        @pl.loop(0, NB)
        def _(i):
            rows = pl.ds(pl.multiple_of(i * RB, RB), RB)
            y = dot(x_ref[rows, :], rot_ref[:, cols]).astype(bf16)
            y_ref[g, rows, :] = y
            yt_ref[g, :, rows] = y.T

    @pl.loop(0, 4)
    def _(i):
        rows = pl.ds(pl.multiple_of(i * 256, 256), 256)
        xt_ref[:, rows] = x_ref[rows, :].T

    for g in range(G):
        factor = s_ref[g] * LOG2E

        @pl.loop(0, NK)
        def _(j):
            ks = pl.ds(pl.multiple_of(j * KC, KC), KC)
            c = cb_ref[g, ks, :]
            ct_ref[g, :, ks] = c.T
            c32 = c.astype(f32)
            sq = jnp.sum(c32 * c32, axis=1, keepdims=True) * factor
            b_ref[g, ks, :] = jnp.broadcast_to(sq, (KC, 128))

    def logits(g, rb, l):
        yt = yt_ref[g, :, pl.ds(rb * RB, RB)]
        scale = s_ref[g] * (2.0 * LOG2E)
        m = None
        for j in range(NK):
            ks = pl.ds(j * KC, KC)
            v = dot(cb_ref[g, ks, :], yt) * scale - jnp.tile(b_ref[g, ks, :], (1, RB // 128))
            l[ks, :] = v
            w = jnp.max(v.reshape(KC // 8, 8, RB), axis=0)
            m = w if m is None else jnp.maximum(m, w)
        return jnp.max(m, axis=0, keepdims=True)

    def softmax(l, m, p, cols):
        tot = None
        for j in range(NK):
            ks = pl.ds(j * KC, KC)
            e = jnp.exp2(l[ks, :] - m)
            w = jnp.sum(e.reshape(KC // 8, 8, RB), axis=0)
            tot = w if tot is None else tot + w
            p[ks, cols] = e.astype(bf16)
        inv = (1.0 / jnp.sum(tot, axis=0, keepdims=True)).astype(bf16)
        for j in range(NK):
            ks = pl.ds(j * KC, KC)
            p[ks, cols] = p[ks, cols] * inv

    def recon(g, rb, p):
        rows = pl.ds(rb * RB, RB)
        recon_ref[rows, pl.ds(g * F, F)] = dot(ct_ref[g], p[:, rows]).T.astype(bf16)

    def sums(g, q, p):
        n = K // NB
        ks = pl.ds(q * n, n)
        pq = p[ks, :]
        sums_ref[g, ks, :] = dot(pq, y_ref[g]).astype(bf16)
        t = pq[:, :128]
        for i in range(1, R // 128):
            t = t + pq[:, i * 128:(i + 1) * 128]
        ones = jnp.ones((8, 128), bf16)
        row = lax.dot_general(ones, t, (((1,), (1,)), ((), ())), preferred_element_type=f32)
        for i in range(4):
            cnt_ref[q, pl.ds(g * 4 + i, 1), :] = row[:1, i * 128:(i + 1) * 128]

    def cross(g):
        cols = pl.ds(g * F, F)
        cross_ref[:, cols] = dot(xt_ref[...], recon_ref[:, cols]).astype(bf16)

    ls, ps = (l0, l1), (p0, p1)
    steps = [(g, rb) for g in range(G) for rb in range(NB)]
    m = logits(0, 0, l0)
    for t, (g, rb) in enumerate(steps):
        nm = logits(*steps[t + 1], ls[(t + 1) % 2]) if t + 1 < len(steps) else None
        softmax(ls[t % 2], m, ps[g % 2], pl.ds(rb * RB, RB))
        if t:
            pg, pr = steps[t - 1]
            recon(pg, pr, ps[pg % 2])
        if g:
            sums(g - 1, rb, ps[(g - 1) % 2])
            if rb == 1:
                cross(g - 1)
        m = nm
    recon(G - 1, NB - 1, ps[(G - 1) % 2])
    for q in range(NB):
        sums(G - 1, q, ps[(G - 1) % 2])
    cross(G - 1)


def compute(s, x, rot, cb):
    return pl.pallas_call(
        compute_kernel,
        out_shape=[
            jax.ShapeDtypeStruct((R, D), bf16),
            jax.ShapeDtypeStruct((G, K, F), bf16),
            jax.ShapeDtypeStruct((4, 16, 128), f32),
            jax.ShapeDtypeStruct((D, D), bf16),
        ],
        in_specs=[pl.BlockSpec(memory_space=pltpu.SMEM), VM, VM, VM],
        out_specs=[VM, VM, VM, VM],
        scratch_shapes=[
            pltpu.VMEM((G, R, F), bf16), pltpu.VMEM((G, F, R), bf16), pltpu.VMEM((D, R), bf16),
            pltpu.VMEM((G, F, K), bf16), pltpu.VMEM((G, K, 128), f32),
            pltpu.VMEM((K, RB), f32), pltpu.VMEM((K, RB), f32),
            pltpu.VMEM((K, R), bf16), pltpu.VMEM((K, R), bf16),
        ],
        compiler_params=pltpu.CompilerParams(vmem_limit_bytes=62 << 20),
        name="soft_assign",
    )(s, x, rot, cb)


REDUCE_COPIES = G * (1 + 6 + 6) + 3 + (1 + 9) + G * (1 + 6 + 6 + 3 + 6 + 6 + 1)


def add(refs):
    total = refs[0].astype(f32)
    for r in refs[1:]:
        total = total + r.astype(f32)
    return total


def reduce_kernel(own_ref, s_ref, n_ref, u_ref, new_ref, out_ref,
                  s0, r0, r1, t1, r2, t2, r3, n0, n1, m1, n2, m2, n3, m3,
                  u0, v0, v1, w1, v2, w2, v3, send, recv, lsem):
    me = Place()
    sems = Sems(send, recv)
    x, y, z, c = me.x, me.y, me.z, me.c
    top, low = pl.ds(0, 32), pl.ds(32, 32)
    left, right = pl.ds(0, 128), pl.ds(128, 128)
    ring = (1, 2, 3)
    me.greet()

    a0 = [sems.copy(s_ref.at[g, :, :, 1 - c], r0.at[g], me.sibling()) for g in range(G)]
    b0 = [sems.copy(u_ref.at[1 - c, :, :, :, pl.ds(g * F, F)], v0.at[g], me.sibling()) for g in range(G)]
    k0 = [sems.copy(n_ref, n0, me.sibling())]

    a1, b1 = [], []
    for g in range(G):
        wait([a0[g]])

        @pl.loop(0, 4)
        def _(i):
            s0[g, i] = add([s_ref[g, i, :, c], r0[g, i]]).astype(bf16)

        a1.append(
            [sems.copy(s0.at[g, me.step("x", d), :, top], r1.at[g, 0, d - 1], me.peer("x", d)) for d in ring]
            + [sems.copy(s0.at[g, :, me.step("z", d), low], r1.at[g, 1, d - 1], me.peer("z", d)) for d in ring]
        )
        wait([b0[g]])

        @pl.loop(0, 4)
        def _(i):
            u0[g, i] = add([u_ref[c, i, :, :, pl.ds(g * F, F)], v0[g, i]]).astype(bf16)

        b1.append(
            [sems.copy(u0.at[g, me.step("x", d), :, :, left], v1.at[g, 0, d - 1], me.peer("x", d)) for d in ring]
            + [sems.copy(u0.at[g, me.step("z", d), :, :, right], v1.at[g, 1, d - 1], me.peer("z", d)) for d in ring]
        )
    wait(k0)
    m1[...] = n_ref[...] + n0[...]
    k1 = [sems.copy(m1.at[me.step("x", d)], n1.at[d - 1], me.peer("x", d)) for d in ring]

    a2, b2 = [], []
    for g in range(G):
        wait(a1[g])
        t1[g, 0] = add([s0[g, x, :, top]] + [r1[g, 0, i] for i in range(3)]).astype(bf16)
        t1[g, 1] = add([s0[g, :, z, low]] + [r1[g, 1, i] for i in range(3)]).astype(bf16)
        a2.append(
            [sems.copy(t1.at[g, 0, me.step("z", d)], r2.at[g, 0, d - 1], me.peer("z", d)) for d in ring]
            + [sems.copy(t1.at[g, 1, me.step("x", d)], r2.at[g, 1, d - 1], me.peer("x", d)) for d in ring]
        )
        wait(b1[g])
        w1[g, 0] = add([u0[g, x, :, :, left]] + [v1[g, 0, i] for i in range(3)]).astype(bf16)
        w1[g, 1] = add([u0[g, z, :, :, right]] + [v1[g, 1, i] for i in range(3)]).astype(bf16)
        b2.append(
            [sems.copy(w1.at[g, 0, me.step("z", d)], v2.at[g, 0, d - 1], me.peer("z", d)) for d in ring]
            + [sems.copy(w1.at[g, 1, me.step("x", d)], v2.at[g, 1, d - 1], me.peer("x", d)) for d in ring]
        )
    wait(k1)
    m2[...] = m1[x] + n1[0] + n1[1] + n1[2]
    k2 = [sems.copy(m2, n2.at[d - 1], me.peer("z", d)) for d in ring]

    b3 = []
    for g in range(G):
        wait(a2[g])
        t2[g, top] = add([t1[g, 0, z]] + [r2[g, 0, i] for i in range(3)]).astype(bf16)
        t2[g, low] = add([t1[g, 1, x]] + [r2[g, 1, i] for i in range(3)]).astype(bf16)
        wait(b2[g])
        v3[g, y, 0] = add([w1[g, 0, z]] + [v2[g, 0, i] for i in range(3)]).astype(bf16)
        v3[g, y, 1] = add([w1[g, 1, x]] + [v2[g, 1, i] for i in range(3)]).astype(bf16)
        b3.append([sems.copy(v3.at[g, y], v3.at[g, y], me.peer("y", d)) for d in ring])
    a3 = [sems.copy(t2.at[me.step("y", d)], r3.at[d - 1], me.peer("y", d)) for d in ring]
    wait(k2)
    m3[...] = m2[...] + n2[0] + n2[1] + n2[2]
    k3 = [sems.copy(m3, n3.at[d - 1], me.peer("y", d)) for d in ring]

    b4 = []
    for g in range(G):
        wait(b3[g])
        one, two = pl.ds(g * F, 128), pl.ds(g * F + 128, 128)
        out_ref[c, x, z, :, one] = add([v3[g, i, 0] for i in range(4)]).astype(bf16)
        out_ref[c, z, x, :, two] = add([v3[g, i, 1] for i in range(4)]).astype(bf16)
        e, f = out_ref.at[c, x, z, :, one], out_ref.at[c, z, x, :, two]
        b4.append(
            [sems.copy(e, e, me.peer("z", d)) for d in ring] + [sems.copy(f, f, me.peer("x", d)) for d in ring]
        )

    wait(a3)
    wait(k3)
    sums = add([t2[y]] + [r3[i] for i in range(3)])
    rows = m3[...] + n3[0] + n3[1] + n3[2]
    at_row = lax.broadcasted_iota(jnp.int32, (16, 128), 0) == y * 4 + z
    row = jnp.sum(jnp.where(at_row, rows, 0.0), axis=0, keepdims=True)
    spread = jnp.broadcast_to(row, (64, 128))
    lane, sub = lax.broadcasted_iota(jnp.int32, (64, 128), 1), lax.broadcasted_iota(jnp.int32, (64, 128), 0)
    count = jnp.sum(jnp.where(lane == sub + c * 64, spread, 0.0), axis=1, keepdims=True)
    new_ref[0] = (sums + own_ref[0].astype(f32)) / (count + 1.0)

    b5 = []
    for g in range(G):
        wait(b4[g])
        one, two = pl.ds(g * F, 128), pl.ds(g * F + 128, 128)
        e, f = out_ref.at[c, x, :, :, one], out_ref.at[c, z, :, :, two]
        b5.append(
            [sems.copy(e, e, me.peer("x", d)) for d in ring] + [sems.copy(f, f, me.peer("z", d)) for d in ring]
        )
    b6 = []
    for g in range(G):
        wait(b5[g])
        e = out_ref.at[c, :, :, :, pl.ds(g * F, F)]
        b6.append(sems.copy(e, e, me.sibling()))
    wait(b6)


def reduce(own, sums, counts, cross):
    return pl.pallas_call(
        reduce_kernel,
        out_shape=[
            jax.ShapeDtypeStruct((1, 64, F), f32),
            jax.ShapeDtypeStruct((2, 4, 4, 32, D), bf16),
        ],
        in_specs=[VM] * 4,
        out_specs=[VM] * 2,
        scratch_shapes=[
            pltpu.VMEM((G, 4, 4, 64, F), bf16), pltpu.VMEM((G, 4, 4, 64, F), bf16),
            pltpu.VMEM((G, 2, 3, 4, 32, F), bf16), pltpu.VMEM((G, 2, 4, 32, F), bf16),
            pltpu.VMEM((G, 2, 3, 32, F), bf16), pltpu.VMEM((G, 64, F), bf16), pltpu.VMEM((3, 64, F), bf16),
            pltpu.VMEM((4, 16, 128), f32), pltpu.VMEM((3, 16, 128), f32), pltpu.VMEM((4, 16, 128), f32),
            pltpu.VMEM((3, 16, 128), f32), pltpu.VMEM((16, 128), f32), pltpu.VMEM((3, 16, 128), f32),
            pltpu.VMEM((16, 128), f32),
            pltpu.VMEM((G, 4, 4, 32, F), bf16), pltpu.VMEM((G, 4, 4, 32, F), bf16),
            pltpu.VMEM((G, 2, 3, 4, 32, 128), bf16), pltpu.VMEM((G, 2, 4, 32, 128), bf16),
            pltpu.VMEM((G, 2, 3, 32, 128), bf16), pltpu.VMEM((16, 128), bf16),
            pltpu.VMEM((G, 4, 2, 32, 128), bf16),
            pltpu.SemaphoreType.DMA((REDUCE_COPIES,)),
            pltpu.SemaphoreType.DMA((REDUCE_COPIES,)),
            pltpu.SemaphoreType.DMA,
        ],
        compiler_params=pltpu.CompilerParams(collective_id=1, has_side_effects=True, vmem_limit_bytes=48 << 20),
        name="reduce_all",
    )(own, sums, counts, cross)


def body(vector_window, orthogonal_matrix, centroid_table, sharpness_scale):
    codewords = gather(centroid_table)
    recon, sums, counts, cross = compute(
        sharpness_scale, vector_window, orthogonal_matrix, codewords.reshape(G, K, F)
    )
    new_codebook, total = reduce(
        centroid_table, sums.reshape(G, 4, 4, 2, 64, F), counts, cross.reshape(2, 4, 4, 32, D)
    )
    total_rows = R * lax.axis_size("dp") * lax.axis_size("sub")
    cross_cov = total.reshape(D, D).astype(f32) * (1.0 / math.sqrt(total_rows))
    return (new_codebook, recon, cross_cov)


def solution(mesh):
    placed = (P(("dp", "sub"), None), P(), P("sub", "dp", None), P())
    return jax.shard_map(
        body,
        mesh=mesh,
        in_specs=placed,
        out_specs=(P("sub", "dp", None), P(("dp", "sub"), None), P()),
        check_vma=False,
    )
```

time: 477 us -> 126 us (0.26)
  waiting for transfers between devices: 340 us -> 0 us
  Pallas kernels: 0 us -> 116 us
  matrix products: 54.3 us -> 0 us
  other arithmetic: 42.4 us -> 2.62 us
  between operations: 13.8 us -> 0.67 us
  starting transfers between devices: 9.8 us -> 0 us
  local copies, waits for them, and re-layouts: 15.2 us -> 5.74 us
    psum x1 -> x0, waiting for transfers between devices: 160 us -> none  [body(): cross_cov = lax.psum(partial_value, ('dp', 'sub')) / math.sqrt(total_rows)]
    pallas_call x0 -> x3, Pallas kernels: none -> 116 us  [the longest x1 47.8 us: reduce(): pl.pallas_call(reduce_kernel, out_shape=[jax.ShapeDtypeStruct((1, 64, F),...]
    reduce_scatter x1 -> x0, waiting for transfers between devices: 79.6 us -> none  [body(): lax.psum_scatter(group_sums.astype(jnp.bfloat16), 'dp', scatter_dimension...]
    dot_general x14 -> x0, matrix products: 54.3 us -> none  [the longest x4 22.6 us: step(): lax.dot_general(probs, block_index, (((0,), (0,)), ((), ())), preferred_e...]
    unnamed x5 -> x0, waiting for transfers between devices: 45.9 us -> none
    all_gather x1 -> x0, waiting for transfers between devices: 33.2 us -> none  [body(): entire_vocabulary = lax.all_gather(centroid_table, 'dp', axis=1, tiled=True)]
    reduce_sum x9 -> x0, other arithmetic: 32.5 us -> none  [the longest x4 18.5 us: step(): jnp.sum(probs.astype(jnp.float32), axis=0)]
    all_to_all x2 -> x0, waiting for transfers between devices: 22.1 us -> none  [the longest x1 22.1 us: body(): lax.all_to_all(restored_vectors, 'sub', split_axis=0, concat_axis=1, tile...]
  transfers between devices with their start and end apart: 6 -> 0, of which waited for: 5 -> 0; matrix products, arithmetic and copies ran while one was open for 5% -> 0% of each run, Pallas kernels for 0% -> 0%
where the time goes in v1:
time: 126 us; the launch traced here: 125 us
  Pallas kernels  116 us (92%)
  local copies, waits for them, and re-layouts  5.74 us (5%)
  other arithmetic  2.62 us (2%)
    pallas_call x1, Pallas kernels, reduce(): pl.pallas_call(reduce_kernel, out_shape=[jax.ShapeDtypeStruct((1, 64, F),...  47.8 us
    pallas_call x1, Pallas kernels, compute(): pl.pallas_call(compute_kernel, out_shape=[jax.ShapeDtypeStruct((R, D), bf...  37.7 us
    pallas_call x1, Pallas kernels, gather(): pl.pallas_call(gather_kernel, out_shape=jax.ShapeDtypeStruct((G, 4, 4, 2,...  30.7 us
    unnamed x11, local copies, waits for them, and re-layouts  5.74 us
    mul x1, other arithmetic, body(): cross_cov = total.reshape(D, D).astype(f32) * (1.0 / math.sqrt(total_rows))  2.62 us

profile of v1, /device:TPU:1, one launch (start us, length us, event | category | flops | bytes accessed | tf_op | source)
XLA Modules:
  0.0 125.3 jit_solution(3025666793469609584)
XLA Ops:
  0.6 0.0 copy-start.2
  0.6 0.7 copy-done.2
  1.4 30.7 %gather_codewords.1 = bf16[4,4,4,2,64,256]{5,4,3,2,1,0:T(8,128)(2,1)S(1)} custom-call(bf16[1,64,256]{2,1,0:T(8,128)(2,1)S(1)} %copy-done.2), custom_call_target="tpu_custom_call" | custom-call | tf_op jit(solution)/shard_map/gather_codewords/pallas_call | solution.py:116
  32.1 0.0 copy-start
  32.1 2.0 %copy-done = bf16[4,4,4,2,64,256]{5,4,3,2,1,0:T(8,128)(2,1)} copy-done((bf16[4,4,4,2,64,256]{5,4,3,2,1,0:T(8,128)(2,1)}, bf16[4,4,4,2,64,256]{5,4,3,2,1,0:T(8,128)(2,1)S(1)}, u32[]{:S(2)}) %copy-start) | copy-done | bytes 4194328
  34.1 0.0 copy-start.3
  34.1 37.7 %soft_assign.1 = (bf16[1024,1024]{1,0:T(8,128)(2,1)}, bf16[4,2048,256]{2,1,0:T(8,128)(2,1)}, f32[4,16,128]{2,1,0:T(8,128)}, bf16[1024,1024]{1,0:T(8,128)(2,1)}) custom-call(f32[4]{0:T(128)} %s_ref.1, bf16[1024,1024]{1,0:T(8,128)(2,1)} %x_ref.1, bf16[1024,1024]{1,0:T(8,128)(2,1)} %rot_ref.1, bf16[4,2048,256]{2,1,0:T(8,128)(2,1)} %bitcast.4), custom_call_target="tpu_custom_call" | custom-call | tf_op jit(solution)/shard_map/soft_assign/pallas_call | solution.py:227
  71.8 0.0 copy-done.3
  71.8 0.0 copy-start.1
  71.8 1.6 %copy-done.1 = bf16[1024,1024]{1,0:T(8,128)(2,1)S(1)} copy-done((bf16[1024,1024]{1,0:T(8,128)(2,1)S(1)}, bf16[1024,1024]{1,0:T(8,128)(2,1)}, u32[]{:S(2)}) %copy-start.1) | copy-done | bytes 2097176
  73.4 0.0 copy-start.4
  73.4 0.8 copy-done.4
  74.2 47.8 %reduce_all.1 = (f32[1,64,256]{2,1,0:T(8,128)S(1)}, bf16[2,4,4,32,1024]{4,3,2,1,0:T(8,128)(2,1)S(1)}) custom-call(bf16[1,64,256]{2,1,0:T(8,128)(2,1)S(1)} %copy-done.3, bf16[4,4,4,2,64,256]{5,4,3,2,1,0:T(8,128)(2,1)} %bitcast.7, f32[4,16,128]{2,1,0:T(8,128)S(1)} %copy-done.4, bf16[2,4,4,32,1024]{4,3,2,1,0:T(8,128)(2,1)S(1)} %bitcast.5), custom_call_target="tpu_custom_call" | custom-call | tf_op jit(solution)/shard_map/reduce_all/pallas_call | solution.py:372
  122.0 2.6 %convert_multiply_fusion = f32[2,4,4,32,1024]{4,3,2,1,0:T(8,128)} fusion(bf16[2,4,4,32,1024]{4,3,2,1,0:T(8,128)(2,1)S(1)} %get-tuple-element.14), kind=kLoop, calls=%fused_computation | loop fusion | flops 2097152 | bytes 6291456 | tf_op jit(solution)/shard_map/mul | solution.py:409
  124.6 0.6 copy.8
Async XLA Ops:
  0.6 0.8 copy-start.2
  32.1 2.0 %copy-start = (bf16[4,4,4,2,64,256]{5,4,3,2,1,0:T(8,128)(2,1)}, bf16[4,4,4,2,64,256]{5,4,3,2,1,0:T(8,128)(2,1)S(1)}, u32[]{:S(2)}) copy-start(bf16[4,4,4,2,64,256]{5,4,3,2,1,0:T(8,128)(2,1)S(1)} %gather_codewords.1) | copy-start | bytes 12582916
  34.1 37.7 %copy-start.3 = (bf16[1,64,256]{2,1,0:T(8,128)(2,1)S(1)}, bf16[1,64,256]{2,1,0:T(8,128)(2,1)}, u32[]{:S(2)}) copy-start(bf16[1,64,256]{2,1,0:T(8,128)(2,1)} %own_ref.3) | copy-start | bytes 98308
  71.8 1.6 %copy-start.1 = (bf16[1024,1024]{1,0:T(8,128)(2,1)S(1)}, bf16[1024,1024]{1,0:T(8,128)(2,1)}, u32[]{:S(2)}) copy-start(bf16[1024,1024]{1,0:T(8,128)(2,1)} %get-tuple-element.11) | copy-start | bytes 6291460
  73.4 0.8 copy-start.4

commit v2 on v0

v2 whole, which is shorter than its diff:
```python
import math

import jax
import jax.numpy as jnp
from jax import lax
from jax.experimental import pallas as pl
from jax.experimental.pallas import tpu as pltpu
from jax.sharding import PartitionSpec as P

LOG2E = math.log2(math.e)
G, F, K, D, R = 4, 256, 2048, 1024, 1024
RB = 256
NB = R // RB
KC = 256
NK = K // KC
f32, bf16 = jnp.float32, jnp.bfloat16
MESH = pl.DeviceIdType.MESH
VM = pl.BlockSpec(memory_space=pltpu.VMEM)


def dot(a, b):
    return jnp.dot(a, b, preferred_element_type=f32)


class Place:
    def __init__(self):
        dp, self.y = lax.axis_index("dp"), lax.axis_index("sub")
        self.x, self.z, self.c = dp // 8, (dp // 2) % 4, dp % 2

    def at(self, axis):
        return {"x": self.x, "y": self.y, "z": self.z}[axis]

    def step(self, axis, d):
        return (self.at(axis) + d) % 4

    def peer(self, axis, d):
        x, y, z = self.x, self.y, self.z
        if axis == "x":
            x = self.step("x", d)
        if axis == "y":
            y = self.step("y", d)
        if axis == "z":
            z = self.step("z", d)
        return ((x * 4 + z) * 2 + self.c, y)

    def sibling(self):
        return ((self.x * 4 + self.z) * 2 + 1 - self.c, self.y)

    def greet(self):
        barrier = pltpu.get_barrier_semaphore()
        for axis in "xyz":
            for d in (1, 2, 3):
                pl.semaphore_signal(barrier, inc=1, device_id=self.peer(axis, d), device_id_type=MESH)
        pl.semaphore_signal(barrier, inc=1, device_id=self.sibling(), device_id_type=MESH)
        pl.semaphore_wait(barrier, 10)


class Sems:
    def __init__(self, send, recv):
        self.send, self.recv, self.n = send, recv, 0

    def copy(self, src, dst, device):
        i = self.n
        self.n += 1
        op = pltpu.make_async_remote_copy(
            src_ref=src, dst_ref=dst, send_sem=self.send.at[i], recv_sem=self.recv.at[i],
            device_id=device, device_id_type=MESH,
        )
        op.start()
        return op


def wait(copies):
    for op in copies:
        op.wait()


RING = (1, 2, 3)
TOP, LOW = pl.ds(0, 32), pl.ds(32, 32)


def add(refs):
    total = refs[0].astype(f32)
    for r in refs[1:]:
        total = total + r.astype(f32)
    return total


def kernel(s_ref, x_hbm, rot_hbm, own_ref, new_ref, recon_hbm, out_ref,
           x_ref, rot_ref, cb_ref, recon_ref, s_sum, u_ref, n_ref,
           y_ref, yt_ref, xt_ref, ct0, ct1, b0, b1, l0, l1, p0, p1,
           s0, r0, r1, t1, r2, t2, r3, n0, n1, m1, n2, m2, n3, m3,
           u0, v0, v1, w1, v2, w2, v3, send, recv, lsem):
    me = Place()
    sems = Sems(send, recv)
    x, y, z, c = me.x, me.y, me.z, me.c

    def to(axis, pairs):
        return [sems.copy(*pairs(d), me.peer(axis, d)) for d in RING]

    load_x = pltpu.make_async_copy(x_hbm, x_ref, lsem.at[0])
    load_rot = pltpu.make_async_copy(rot_hbm, rot_ref, lsem.at[1])
    mine = pltpu.make_async_copy(own_ref.at[0], cb_ref.at[y, x, z, c], lsem.at[2])
    load_x.start()
    load_rot.start()
    mine.start()
    me.greet()


    def gather_own():
        return to("y", lambda d: (own_ref.at[0], cb_ref.at[y, x, z, c]))

    def gather_first(g):
        a, b = cb_ref.at[g, x, z, c, TOP], cb_ref.at[g, x, z, c, LOW]
        return to("x", lambda d: (a, a)) + to("z", lambda d: (b, b))

    def gather_second(g):
        a, b = cb_ref.at[g, :, z, c, TOP], cb_ref.at[g, x, :, c, LOW]
        return to("z", lambda d: (a, a)) + to("x", lambda d: (b, b))

    def gather_core(g):
        a = cb_ref.at[g, :, :, c]
        return [sems.copy(a, a, me.sibling())]

    def sums_task(g):
        ops = [sems.copy(s_sum.at[g, :, :, 1 - c], r0.at[g], me.sibling())]
        yield
        wait(ops)

        @pl.loop(0, 4)
        def _(i):
            s0[g, i] = add([s_sum[g, i, :, c], r0[g, i]]).astype(bf16)

        ops = to("x", lambda d: (s0.at[g, me.step("x", d), :, TOP], r1.at[g, 0, d - 1]))
        ops += to("z", lambda d: (s0.at[g, :, me.step("z", d), LOW], r1.at[g, 1, d - 1]))
        yield
        wait(ops)
        t1[g, 0] = add([s0[g, x, :, TOP]] + [r1[g, 0, i] for i in range(3)]).astype(bf16)
        t1[g, 1] = add([s0[g, :, z, LOW]] + [r1[g, 1, i] for i in range(3)]).astype(bf16)
        ops = to("z", lambda d: (t1.at[g, 0, me.step("z", d)], r2.at[g, 0, d - 1]))
        ops += to("x", lambda d: (t1.at[g, 1, me.step("x", d)], r2.at[g, 1, d - 1]))
        yield
        wait(ops)
        t2[g, TOP] = add([t1[g, 0, z]] + [r2[g, 0, i] for i in range(3)]).astype(bf16)
        t2[g, LOW] = add([t1[g, 1, x]] + [r2[g, 1, i] for i in range(3)]).astype(bf16)

    def counts_task():
        ops = [sems.copy(n_ref, n0, me.sibling())]
        yield
        wait(ops)
        m1[...] = n_ref[...] + n0[...]
        ops = to("x", lambda d: (m1.at[me.step("x", d)], n1.at[d - 1]))
        yield
        wait(ops)
        m2[...] = m1[x] + n1[0] + n1[1] + n1[2]
        ops = to("z", lambda d: (m2, n2.at[d - 1]))
        yield
        wait(ops)
        m3[...] = m2[...] + n2[0] + n2[1] + n2[2]

    def owner_task():
        ops = to("y", lambda d: (t2.at[me.step("y", d)], r3.at[d - 1]))
        ops += to("y", lambda d: (m3, n3.at[d - 1]))
        yield
        wait(ops)
        sums = add([t2[y]] + [r3[i] for i in range(3)])
        rows = m3[...] + n3[0] + n3[1] + n3[2]
        at_row = lax.broadcasted_iota(jnp.int32, (16, 128), 0) == y * 4 + z
        row = jnp.sum(jnp.where(at_row, rows, 0.0), axis=0, keepdims=True)
        spread = jnp.broadcast_to(row, (64, 128))
        lane, sub = lax.broadcasted_iota(jnp.int32, (64, 128), 1), lax.broadcasted_iota(jnp.int32, (64, 128), 0)
        count = jnp.sum(jnp.where(lane == sub + c * 64, spread, 0.0), axis=1, keepdims=True)
        new_ref[0] = (sums + own_ref[0].astype(f32)) / (count + 1.0)

    def cross_task(g):
        one, two = pl.ds(g * F, 128), pl.ds(g * F + 128, 128)
        left, right = pl.ds(0, 128), pl.ds(128, 128)
        ops = [sems.copy(u_ref.at[1 - c, :, :, :, pl.ds(g * F, F)], v0.at[g], me.sibling())]
        yield
        wait(ops)

        @pl.loop(0, 4)
        def _(i):
            u0[g, i] = add([u_ref[c, i, :, :, pl.ds(g * F, F)], v0[g, i]]).astype(bf16)

        ops = to("x", lambda d: (u0.at[g, me.step("x", d), :, :, left], v1.at[g, 0, d - 1]))
        ops += to("z", lambda d: (u0.at[g, me.step("z", d), :, :, right], v1.at[g, 1, d - 1]))
        yield
        wait(ops)
        w1[g, 0] = add([u0[g, x, :, :, left]] + [v1[g, 0, i] for i in range(3)]).astype(bf16)
        w1[g, 1] = add([u0[g, z, :, :, right]] + [v1[g, 1, i] for i in range(3)]).astype(bf16)
        ops = to("z", lambda d: (w1.at[g, 0, me.step("z", d)], v2.at[g, 0, d - 1]))
        ops += to("x", lambda d: (w1.at[g, 1, me.step("x", d)], v2.at[g, 1, d - 1]))
        yield
        wait(ops)
        v3[g, y, 0] = add([w1[g, 0, z]] + [v2[g, 0, i] for i in range(3)]).astype(bf16)
        v3[g, y, 1] = add([w1[g, 1, x]] + [v2[g, 1, i] for i in range(3)]).astype(bf16)
        ops = to("y", lambda d: (v3.at[g, y], v3.at[g, y]))
        yield
        wait(ops)
        out_ref[c, x, z, :, one] = add([v3[g, i, 0] for i in range(4)]).astype(bf16)
        out_ref[c, z, x, :, two] = add([v3[g, i, 1] for i in range(4)]).astype(bf16)
        e, f = out_ref.at[c, x, z, :, one], out_ref.at[c, z, x, :, two]
        ops = to("z", lambda d: (e, e)) + to("x", lambda d: (f, f))
        yield
        wait(ops)
        h, i = out_ref.at[c, x, :, :, one], out_ref.at[c, z, :, :, two]
        ops = to("x", lambda d: (h, h)) + to("z", lambda d: (i, i))
        yield
        wait(ops)
        k = out_ref.at[c, :, :, :, pl.ds(g * F, F)]
        ops = [sems.copy(k, k, me.sibling())]
        yield
        wait(ops)


    cts, bs, ls, ps = (ct0, ct1), (b0, b1), (l0, l1), (p0, p1)

    def rotate():
        @pl.loop(0, NB)
        def _(i):
            rows = pl.ds(pl.multiple_of(i * RB, RB), RB)
            for g in range(G):
                v = dot(x_ref[rows, :], rot_ref[:, pl.ds(g * F, F)]).astype(bf16)
                y_ref[g, rows, :] = v
                yt_ref[g, :, rows] = v.T

    def turn_x():
        @pl.loop(0, 4)
        def _(i):
            rows = pl.ds(pl.multiple_of(i * 256, 256), 256)
            xt_ref[:, rows] = x_ref[rows, :].T

    def words(g, j):
        return cb_ref[g, j // 2, pl.ds((j % 2) * 2, 2)].reshape(KC, F)

    def prepare(g):
        factor = s_ref[g] * LOG2E
        for j in range(NK):
            ks = pl.ds(j * KC, KC)
            v = words(g, j)
            cts[g % 2][:, ks] = v.T
            v32 = v.astype(f32)
            sq = jnp.sum(v32 * v32, axis=1, keepdims=True) * factor
            bs[g % 2][ks, :] = jnp.broadcast_to(sq, (KC, 128))

    def logits(g, rb, l):
        yt = yt_ref[g, :, pl.ds(rb * RB, RB)]
        scale = s_ref[g] * (2.0 * LOG2E)
        m = None
        for j in range(NK):
            ks = pl.ds(j * KC, KC)
            v = dot(words(g, j), yt) * scale - jnp.tile(bs[g % 2][ks, :], (1, RB // 128))
            l[ks, :] = v
            w = jnp.max(v.reshape(KC // 8, 8, RB), axis=0)
            m = w if m is None else jnp.maximum(m, w)
        return jnp.max(m, axis=0, keepdims=True)

    def softmax(l, m, p, cols):
        tot = None
        for j in range(NK):
            ks = pl.ds(j * KC, KC)
            e = jnp.exp2(l[ks, :] - m)
            w = jnp.sum(e.reshape(KC // 8, 8, RB), axis=0)
            tot = w if tot is None else tot + w
            p[ks, cols] = e.astype(bf16)
        inv = (1.0 / jnp.sum(tot, axis=0, keepdims=True)).astype(bf16)
        for j in range(NK):
            ks = pl.ds(j * KC, KC)
            p[ks, cols] = p[ks, cols] * inv

    def recon(g, rb, p):
        rows = pl.ds(rb * RB, RB)
        recon_ref[rows, pl.ds(g * F, F)] = dot(cts[g % 2][...], p[:, rows]).T.astype(bf16)

    def sums(g, q, p):
        n = K // NB
        pq = p[pl.ds(q * n, n), :]
        s_sum[g, q] = dot(pq, y_ref[g]).astype(bf16).reshape(4, 2, 64, F)
        t = pq[:, :128]
        for i in range(1, R // 128):
            t = t + pq[:, i * 128:(i + 1) * 128]
        ones = jnp.ones((8, 128), bf16)
        row = lax.dot_general(ones, t, (((1,), (1,)), ((), ())), preferred_element_type=f32)
        for i in range(4):
            n_ref[q, pl.ds(g * 4 + i, 1), :] = row[:1, i * 128:(i + 1) * 128]

    def cross(g):
        cols = pl.ds(g * F, F)
        u_ref[:, :, :, :, cols] = dot(xt_ref[...], recon_ref[:, cols]).astype(bf16).reshape(2, 4, 4, 32, F)

    def store(g):
        cols = pl.ds(g * F, F)
        op = pltpu.make_async_copy(recon_ref.at[:, cols], recon_hbm.at[:, cols], lsem.at[3 + g])
        op.start()
        return op


    stage_y = gather_own()
    load_x.wait()
    load_rot.wait()
    mine.wait()
    wait(stage_y)
    first = [gather_first(0)]
    rotate()
    wait(first[0])
    second = [gather_second(0)]
    first.append(gather_first(1))
    turn_x()
    wait(first[1])
    wait(second[0])
    last = [gather_core(0)]
    second.append(gather_second(1))
    first.append(gather_first(2))
    wait(last[0])
    prepare(0)

    stores, tasks = [], []

    def tick(now):
        for task in list(tasks):
            if now >= task[1]:
                task[1] = now + 2
                if next(task[0], task) is task:
                    tasks.remove(task)

    def begin(now, task):
        tasks.append([task, now + 2])
        next(task)

    steps = [(g, rb) for g in range(G) for rb in range(NB)]
    m = logits(0, 0, l0)
    for t, (g, rb) in enumerate(steps):
        if g + 1 < G:
            if rb == 1:
                wait(second[g + 1])
                last.append(gather_core(g + 1))
                if g + 2 < G:
                    wait(first[g + 2])
                    second.append(gather_second(g + 2))
                if g + 3 < G:
                    first.append(gather_first(g + 3))
            if rb == 2:
                wait(last[g + 1])
                prepare(g + 1)
        nm = logits(*steps[t + 1], ls[(t + 1) % 2]) if t + 1 < len(steps) else None
        softmax(ls[t % 2], m, ps[g % 2], pl.ds(rb * RB, RB))
        if t:
            pg, pr = steps[t - 1]
            recon(pg, pr, ps[pg % 2])
        if g:
            sums(g - 1, rb, ps[(g - 1) % 2])
            if rb == 0:
                stores.append(store(g - 1))
                cross(g - 1)
        tick(t)
        if g and rb == 0:
            begin(t, cross_task(g - 1))
        if g and rb == 3:
            begin(t, sums_task(g - 1))
        m = nm
    recon(G - 1, NB - 1, ps[(G - 1) % 2])
    stores.append(store(G - 1))
    cross(G - 1)
    begin(0, cross_task(G - 1))
    for q in range(NB):
        sums(G - 1, q, ps[(G - 1) % 2])
    begin(0, sums_task(G - 1))
    begin(0, counts_task())
    reduced = [task for task in tasks]
    owner = None
    while tasks:
        tick(1 << 20)
        for task in tasks:
            task[1] = 0
        if owner is None and not any(t in tasks for t in reduced[-2:]):
            owner = owner_task()
            begin(0, owner)
    for op in stores:
        op.wait()


COPIES = 3 + G * 13 + G * 13 + 10 + 6 + G * 29


def call(s, x, rot, own):
    any_place = pl.BlockSpec(memory_space=pl.ANY)
    return pl.pallas_call(
        kernel,
        out_shape=[
            jax.ShapeDtypeStruct((1, 64, F), f32),
            jax.ShapeDtypeStruct((R, D), bf16),
            jax.ShapeDtypeStruct((2, 4, 4, 32, D), bf16),
        ],
        in_specs=[pl.BlockSpec(memory_space=pltpu.SMEM), any_place, any_place, VM],
        out_specs=[VM, any_place, VM],
        scratch_shapes=[
            pltpu.VMEM((R, D), bf16), pltpu.VMEM((D, D), bf16), pltpu.VMEM((G, 4, 4, 2, 64, F), bf16),
            pltpu.VMEM((R, D), bf16), pltpu.VMEM((G, 4, 4, 2, 64, F), bf16), pltpu.VMEM((2, 4, 4, 32, D), bf16),
            pltpu.VMEM((4, 16, 128), f32),
            pltpu.VMEM((G, R, F), bf16), pltpu.VMEM((G, F, R), bf16), pltpu.VMEM((D, R), bf16),
            pltpu.VMEM((F, K), bf16), pltpu.VMEM((F, K), bf16),
            pltpu.VMEM((K, 128), f32), pltpu.VMEM((K, 128), f32),
            pltpu.VMEM((K, RB), f32), pltpu.VMEM((K, RB), f32),
            pltpu.VMEM((K, R), bf16), pltpu.VMEM((K, R), bf16),
            pltpu.VMEM((G, 4, 4, 64, F), bf16), pltpu.VMEM((G, 4, 4, 64, F), bf16),
            pltpu.VMEM((G, 2, 3, 4, 32, F), bf16), pltpu.VMEM((G, 2, 4, 32, F), bf16),
            pltpu.VMEM((G, 2, 3, 32, F), bf16), pltpu.VMEM((G, 64, F), bf16), pltpu.VMEM((3, 64, F), bf16),
            pltpu.VMEM((4, 16, 128), f32), pltpu.VMEM((3, 16, 128), f32), pltpu.VMEM((4, 16, 128), f32),
            pltpu.VMEM((3, 16, 128), f32), pltpu.VMEM((16, 128), f32), pltpu.VMEM((3, 16, 128), f32),
            pltpu.VMEM((16, 128), f32),
            pltpu.VMEM((G, 4, 4, 32, F), bf16), pltpu.VMEM((G, 4, 4, 32, F), bf16),
            pltpu.VMEM((G, 2, 3, 4, 32, 128), bf16), pltpu.VMEM((G, 2, 4, 32, 128), bf16),
            pltpu.VMEM((G, 2, 3, 32, 128), bf16), pltpu.VMEM((16, 128), bf16),
            pltpu.VMEM((G, 4, 2, 32, 128), bf16),
            pltpu.SemaphoreType.DMA((COPIES,)),
            pltpu.SemaphoreType.DMA((COPIES,)),
            pltpu.SemaphoreType.DMA((3 + G,)),
        ],
        compiler_params=pltpu.CompilerParams(collective_id=0, has_side_effects=True, vmem_limit_bytes=63 << 20),
        name="quantizer_step",
    )(s, x, rot, own)


def body(vector_window, orthogonal_matrix, centroid_table, sharpness_scale):
    new_codebook, recon, total = call(sharpness_scale, vector_window, orthogonal_matrix, centroid_table)
    total_rows = R * lax.axis_size("dp") * lax.axis_size("sub")
    cross_cov = total.reshape(D, D).astype(f32) * (1.0 / math.sqrt(total_rows))
    return (new_codebook, recon, cross_cov)


def solution(mesh):
    placed = (P(("dp", "sub"), None), P(), P("sub", "dp", None), P())
    return jax.shard_map(
        body,
        mesh=mesh,
        in_specs=placed,
        out_specs=(P("sub", "dp", None), P(("dp", "sub"), None), P()),
        check_vma=False,
    )
```

time: 477 us -> 100 us (0.21)
  waiting for transfers between devices: 340 us -> 0 us
  Pallas kernels: 0 us -> 93.2 us
  matrix products: 54.3 us -> 0 us
  other arithmetic: 42.4 us -> 4.35 us
  local copies, waits for them, and re-layouts: 15.2 us -> 1.96 us
  between operations: 13.8 us -> 0.66 us
  starting transfers between devices: 9.8 us -> 0 us
    psum x1 -> x0, waiting for transfers between devices: 160 us -> none  [body(): cross_cov = lax.psum(partial_value, ('dp', 'sub')) / math.sqrt(total_rows)]
    pallas_call x0 -> x1, Pallas kernels: none -> 93.2 us  [call(): pl.pallas_call(kernel, out_shape=[jax.ShapeDtypeStruct((1, 64, F), f32),...]
    reduce_scatter x1 -> x0, waiting for transfers between devices: 79.6 us -> none  [body(): lax.psum_scatter(group_sums.astype(jnp.bfloat16), 'dp', scatter_dimension...]
    dot_general x14 -> x0, matrix products: 54.3 us -> none  [the longest x4 22.6 us: step(): lax.dot_general(probs, block_index, (((0,), (0,)), ((), ())), preferred_e...]
    unnamed x5 -> x0, waiting for transfers between devices: 45.9 us -> none
    all_gather x1 -> x0, waiting for transfers between devices: 33.2 us -> none  [body(): entire_vocabulary = lax.all_gather(centroid_table, 'dp', axis=1, tiled=True)]
    reduce_sum x9 -> x0, other arithmetic: 32.5 us -> none  [the longest x4 18.5 us: step(): jnp.sum(probs.astype(jnp.float32), axis=0)]
    all_to_all x2 -> x0, waiting for transfers between devices: 22.1 us -> none  [the longest x1 22.1 us: body(): lax.all_to_all(restored_vectors, 'sub', split_axis=0, concat_axis=1, tile...]
  transfers between devices with their start and end apart: 6 -> 0, of which waited for: 5 -> 0; matrix products, arithmetic and copies ran while one was open for 5% -> 0% of each run, Pallas kernels for 0% -> 0%
where the time goes in v2:
time: 100 us
  Pallas kernels  93.2 us (93%)
  other arithmetic  4.35 us (4%)
  local copies, waits for them, and re-layouts  1.96 us (2%)
    pallas_call x1, Pallas kernels, call(): pl.pallas_call(kernel, out_shape=[jax.ShapeDtypeStruct((1, 64, F), f32),...  93.2 us
    mul x1, other arithmetic, body(): cross_cov = total.reshape(D, D).astype(f32) * (1.0 / math.sqrt(total_rows))  4.35 us

profile of v2, /device:TPU:1, one launch (start us, length us, event | category | flops | bytes accessed | tf_op | source)
XLA Modules:
  0.0 100.1 jit_solution(14564737326462321119)
XLA Ops:
  0.6 93.2 %quantizer_step.1 = (f32[1,64,256]{2,1,0:T(8,128)}, bf16[1024,1024]{1,0:T(8,128)(2,1)}, bf16[2,4,4,32,1024]{4,3,2,1,0:T(8,128)(2,1)}) custom-call(f32[4]{0:T(128)} %s_ref.1, bf16[1024,1024]{1,0:T(8,128)(2,1)} %x_hbm.1, bf16[1024,1024]{1,0:T(8,128)(2,1)} %rot_hbm.1, bf16[1,64,256]{2,1,0:T(8,128)(2,1)} %own_ref.1), custom_call_target="tpu_custom_call" | custom-call | tf_op jit(solution)/shard_map/quantizer_step/pallas_call | solution.py:388
  93.8 0.0 copy-start.1
  93.8 0.0 copy-start
  93.8 4.4 %convert_multiply_fusion = f32[2,4,4,32,1024]{4,3,2,1,0:T(8,128)} fusion(bf16[2,4,4,32,1024]{4,3,2,1,0:T(8,128)(2,1)} %get-tuple-element.8), kind=kLoop, calls=%fused_computation | loop fusion | flops 2097152 | bytes 6291456 | tf_op jit(solution)/shard_map/mul | solution.py:428
  98.2 0.0 copy-done.1
  98.2 0.6 copy.9
  98.8 0.0 copy-done
  98.8 1.3 %copy.10 = bf16[1024,1024]{1,0:T(8,128)(2,1)} copy(bf16[1024,1024]{1,0:T(8,128)(2,1)S(1)} %copy-done) | data formatting | bytes 4194304
Async XLA Ops:
  93.8 4.4 %copy-start.1 = (f32[1,64,256]{2,1,0:T(8,128)S(1)}, f32[1,64,256]{2,1,0:T(8,128)}, u32[]{:S(2)}) copy-start(f32[1,64,256]{2,1,0:T(8,128)} %get-tuple-element.12) | copy-start | bytes 196612
  93.8 5.0 %copy-start = (bf16[1024,1024]{1,0:T(8,128)(2,1)S(1)}, bf16[1024,1024]{1,0:T(8,128)(2,1)}, u32[]{:S(2)}) copy-start(bf16[1024,1024]{1,0:T(8,128)(2,1)} %get-tuple-element.13) | copy-start | bytes 6291460

commit v3 on v2

--- a/solution.py
+++ b/solution.py
@@ -1,3 +1,4 @@
+import functools
 import math
 
 import jax
@@ -86,8 +87,8 @@
     return total
 
 
-def kernel(s_ref, x_hbm, rot_hbm, own_ref, new_ref, recon_hbm, out_ref,
-           x_ref, rot_ref, cb_ref, recon_ref, s_sum, u_ref, n_ref,
+def kernel(s_ref, x_hbm, rot_hbm, own_ref, new_ref, recon_ref, out_ref,
+           rot_ref, cb_ref, s_sum, u_ref, n_ref,
            y_ref, yt_ref, xt_ref, ct0, ct1, b0, b1, l0, l1, p0, p1,
            s0, r0, r1, t1, r2, t2, r3, n0, n1, m1, n2, m2, n3, m3,
            u0, v0, v1, w1, v2, w2, v3, send, recv, lsem):
@@ -98,6 +99,7 @@
     def to(axis, pairs):
         return [sems.copy(*pairs(d), me.peer(axis, d)) for d in RING]
 
+    x_ref = recon_ref
     load_x = pltpu.make_async_copy(x_hbm, x_ref, lsem.at[0])
     load_rot = pltpu.make_async_copy(rot_hbm, rot_ref, lsem.at[1])
     mine = pltpu.make_async_copy(own_ref.at[0], cb_ref.at[y, x, z, c], lsem.at[2])
@@ -288,12 +290,6 @@
     def cross(g):
         cols = pl.ds(g * F, F)
         u_ref[:, :, :, :, cols] = dot(xt_ref[...], recon_ref[:, cols]).astype(bf16).reshape(2, 4, 4, 32, F)
-
-    def store(g):
-        cols = pl.ds(g * F, F)
-        op = pltpu.make_async_copy(recon_ref.at[:, cols], recon_hbm.at[:, cols], lsem.at[3 + g])
-        op.start()
-        return op
 
 
     stage_y = gather_own()
@@ -315,18 +311,20 @@
     wait(last[0])
     prepare(0)
 
-    stores, tasks = [], []
+    tasks = []
+
+    def begin(now, task, dues):
+        next(task)
+        tasks.append([task, now + dues[0], dues[1:]])
 
     def tick(now):
-        for task in list(tasks):
-            if now >= task[1]:
-                task[1] = now + 2
-                if next(task[0], task) is task:
-                    tasks.remove(task)
-
-    def begin(now, task):
-        tasks.append([task, now + 2])
-        next(task)
+        for entry in list(tasks):
+            task, due, dues = entry
+            if now >= due:
+                if next(task, task) is task:
+                    tasks.remove(entry)
+                else:
+                    entry[1], entry[2] = now + dues[0], dues[1:]
 
     steps = [(g, rb) for g in range(G) for rb in range(NB)]
     m = logits(0, 0, l0)
@@ -348,36 +346,67 @@
         if t:
             pg, pr = steps[t - 1]
             recon(pg, pr, ps[pg % 2])
-        if g:
+        if g and g < G - 1:
             sums(g - 1, rb, ps[(g - 1) % 2])
-            if rb == 0:
-                stores.append(store(g - 1))
-                cross(g - 1)
+        if g and rb == 0:
+            cross(g - 1)
         tick(t)
         if g and rb == 0:
-            begin(t, cross_task(g - 1))
-        if g and rb == 3:
-            begin(t, sums_task(g - 1))
+            begin(t, cross_task(g - 1), (1, 3, 2, 2, 2, 3, 1))
+        if g and g < G - 1 and rb == 3:
+            begin(t, sums_task(g - 1), (2, 4, 3))
         m = nm
+
     recon(G - 1, NB - 1, ps[(G - 1) % 2])
-    stores.append(store(G - 1))
     cross(G - 1)
-    begin(0, cross_task(G - 1))
+    late = 1 << 20
+    chain = cross_task(G - 1)
+    next(chain)
+    for q in range(NB):
+        sums(G - 2, q, ps[(G - 2) % 2])
+    one = sums_task(G - 2)
+    next(one)
+    next(chain)
+    tick(late)
     for q in range(NB):
         sums(G - 1, q, ps[(G - 1) % 2])
-    begin(0, sums_task(G - 1))
-    begin(0, counts_task())
-    reduced = [task for task in tasks]
-    owner = None
+    two, count = sums_task(G - 1), counts_task()
+    next(two)
+    next(count)
+    next(one)
+    next(count)
+    next(chain)
+    next(two)
+    for entry in tasks:
+        entry[1] = 0
+    tick(late)
+    next(count)
+    next(chain)
+    next(one)
+    for entry in tasks:
+        entry[1] = 0
+    tick(late)
+    next(count, None)
+    next(chain)
+    next(two)
+    next(one, None)
+    for entry in tasks:
+        entry[1] = 0
+    tick(late)
+    next(chain)
+    next(two, None)
+    owner = owner_task()
+    next(owner)
+    for entry in tasks:
+        entry[1] = 0
+    tick(late)
+    next(chain)
     while tasks:
-        tick(1 << 20)
-        for task in tasks:
-            task[1] = 0
-        if owner is None and not any(t in tasks for t in reduced[-2:]):
-            owner = owner_task()
-            begin(0, owner)
-    for op in stores:
-        op.wait()
+        for entry in tasks:
+            entry[1] = 0
+        tick(late)
+    next(owner, None)
+    next(chain, None)
 
 
 COPIES = 3 + G * 13 + G * 13 + 10 + 6 + G * 29
@@ -388,15 +417,15 @@
     return pl.pallas_call(
         kernel,
         out_shape=[
-            jax.ShapeDtypeStruct((1, 64, F), f32),
-            jax.ShapeDtypeStruct((R, D), bf16),
-            jax.ShapeDtypeStruct((2, 4, 4, 32, D), bf16),
+            pltpu.VMEM((1, 64, F), f32),
+            pltpu.VMEM((R, D), bf16),
+            pltpu.VMEM((2, 4, 4, 32, D), bf16),
         ],
         in_specs=[pl.BlockSpec(memory_space=pltpu.SMEM), any_place, any_place, VM],
-        out_specs=[VM, any_place, VM],
+        out_specs=[VM, VM, VM],
         scratch_shapes=[
-            pltpu.VMEM((R, D), bf16), pltpu.VMEM((D, D), bf16), pltpu.VMEM((G, 4, 4, 2, 64, F), bf16),
-            pltpu.VMEM((R, D), bf16), pltpu.VMEM((G, 4, 4, 2, 64, F), bf16), pltpu.VMEM((2, 4, 4, 32, D), bf16),
+            pltpu.VMEM((D, D), bf16), pltpu.VMEM((G, 4, 4, 2, 64, F), bf16),
+            pltpu.VMEM((G, 4, 4, 2, 64, F), bf16), pltpu.VMEM((2, 4, 4, 32, D), bf16),
             pltpu.VMEM((4, 16, 128), f32),
             pltpu.VMEM((G, R, F), bf16), pltpu.VMEM((G, F, R), bf16), pltpu.VMEM((D, R), bf16),
             pltpu.VMEM((F, K), bf16), pltpu.VMEM((F, K), bf16),
@@ -415,18 +444,52 @@
             pltpu.VMEM((G, 4, 2, 32, 128), bf16),
             pltpu.SemaphoreType.DMA((COPIES,)),
             pltpu.SemaphoreType.DMA((COPIES,)),
-            pltpu.SemaphoreType.DMA((3 + G,)),
+            pltpu.SemaphoreType.DMA((3,)),
         ],
-        compiler_params=pltpu.CompilerParams(collective_id=0, has_side_effects=True, vmem_limit_bytes=63 << 20),
+        compiler_params=pltpu.CompilerParams(collective_id=0, has_side_effects=True, vmem_limit_bytes=58 << 20),
         name="quantizer_step",
     )(s, x, rot, own)
+
+
+def finish_kernel(scale, new_in, recon_in, total_in, new_out, recon_out, cross_out, buf, sem):
+    moves = [
+        pltpu.make_async_copy(new_in, new_out, sem.at[0]),
+        pltpu.make_async_copy(recon_in, recon_out, sem.at[1]),
+    ]
+    for op in moves:
+        op.start()
+    n = D // 4
+    for i in range(4):
+        rows = pl.ds(i * n, n)
+        buf[rows, :] = total_in[rows, :].astype(f32) * scale
+        op = pltpu.make_async_copy(buf.at[rows, :], cross_out.at[rows, :], sem.at[2 + i])
+        op.start()
+        moves.append(op)
+    for op in moves:
+        op.wait()
+
+
+def finish(new, recon, total, scale):
+    any_place = pl.BlockSpec(memory_space=pl.ANY)
+    return pl.pallas_call(
+        functools.partial(finish_kernel, scale),
+        out_shape=[
+            jax.ShapeDtypeStruct((1, 64, F), f32),
+            jax.ShapeDtypeStruct((R, D), bf16),
+            jax.ShapeDtypeStruct((D, D), f32),
+        ],
+        in_specs=[VM] * 3,
+        out_specs=[any_place] * 3,
+        scratch_shapes=[pltpu.VMEM((D, D), f32), pltpu.SemaphoreType.DMA((6,))],
+        compiler_params=pltpu.CompilerParams(vmem_limit_bytes=16 << 20),
+        name="write_results",
+    )(new, recon, total)
 
 
 def body(vector_window, orthogonal_matrix, centroid_table, sharpness_scale):
     new_codebook, recon, total = call(sharpness_scale, vector_window, orthogonal_matrix, centroid_table)
     total_rows = R * lax.axis_size("dp") * lax.axis_size("sub")
-    cross_cov = total.reshape(D, D).astype(f32) * (1.0 / math.sqrt(total_rows))
-    return (new_codebook, recon, cross_cov)
+    return tuple(finish(new_codebook, recon, total.reshape(D, D), 1.0 / math.sqrt(total_rows)))
 
 
 def solution(mesh):

time: 100 us -> 89.3 us (0.89)
  Pallas kernels: 93.2 us -> 88.3 us
  other arithmetic: 4.35 us -> 0 us
  local copies, waits for them, and re-layouts: 1.96 us -> 0 us
    pallas_call x1 -> x2, Pallas kernels: 93.2 us -> 88.3 us  [the longest x1 85.6 us: call(): pl.pallas_call(kernel, out_shape=[pltpu.VMEM((1, 64, F), f32), pltpu.VMEM...]
    mul x1 -> x0, other arithmetic: 4.35 us -> none  [body(): cross_cov = total.reshape(D, D).astype(f32) * (1.0 / math.sqrt(total_rows))]
    unnamed x6 -> x0, local copies, waits for them, and re-layouts: 1.96 us -> none
where the time goes in v3:
time: 89.3 us; the launch traced here: 89.2 us
  Pallas kernels  88.3 us (99%)
    pallas_call x1, Pallas kernels, call(): pl.pallas_call(kernel, out_shape=[pltpu.VMEM((1, 64, F), f32), pltpu.VMEM...  85.6 us
    pallas_call x1, Pallas kernels, finish(): pl.pallas_call(functools.partial(finish_kernel, scale), out_shape=[jax.Sh...  2.74 us

profile of v3, /device:TPU:1, one launch (start us, length us, event | category | flops | bytes accessed | tf_op | source)
XLA Modules:
  0.0 89.2 jit_solution(9621428415069872652)
XLA Ops:
  0.6 85.6 %quantizer_step.1 = (f32[1,64,256]{2,1,0:T(8,128)S(1)}, bf16[1024,1024]{1,0:T(8,128)(2,1)S(1)}, bf16[2,4,4,32,1024]{4,3,2,1,0:T(8,128)(2,1)S(1)}) custom-call(f32[4]{0:T(128)} %s_ref.1, bf16[1024,1024]{1,0:T(8,128)(2,1)} %x_hbm.1, bf16[1024,1024]{1,0:T(8,128)(2,1)} %rot_hbm.1, bf16[1,64,256]{2,1,0:T(8,128)(2,1)} %own_ref.1), custom_call_target="tpu_custom_call" | custom-call | tf_op jit(solution)/shard_map/quantizer_step/pallas_call | solution.py:417
  86.2 2.7 %write_results.1 = (f32[1,64,256]{2,1,0:T(8,128)}, bf16[1024,1024]{1,0:T(8,128)(2,1)}, f32[1024,1024]{1,0:T(8,128)}) custom-call(f32[1,64,256]{2,1,0:T(8,128)S(1)} %get-tuple-element.6.new_in, bf16[1024,1024]{1,0:T(8,128)(2,1)S(1)} %get-tuple-element.7.recon_in, bf16[1024,1024]{1,0:T(8,128)(2,1)S(1)} %bitcast.1), custom_call_target="tpu_custom_call" | custom-call | tf_op jit(solution)/shard_map/write_results/pallas_call | solution.py:474

commit v4 on v3

--- a/solution.py
+++ b/solution.py
@@ -91,7 +91,7 @@
            rot_ref, cb_ref, s_sum, u_ref, n_ref,
            y_ref, yt_ref, xt_ref, ct0, ct1, b0, b1, l0, l1, p0, p1,
            s0, r0, r1, t1, r2, t2, r3, n0, n1, m1, n2, m2, n3, m3,
-           u0, v0, v1, w1, v2, w2, v3, send, recv, lsem):
+           u0, v0, v1, v2, v3, send, recv, lsem):
     me = Place()
     sems = Sems(send, recv)
     x, y, z, c = me.x, me.y, me.z, me.c
@@ -175,39 +175,40 @@
         new_ref[0] = (sums + own_ref[0].astype(f32)) / (count + 1.0)
 
     def cross_task(g):
-        one, two = pl.ds(g * F, 128), pl.ds(g * F + 128, 128)
-        left, right = pl.ds(0, 128), pl.ds(128, 128)
+        halves = [(0, ("x", "z", "y")), (1, ("z", "y", "x"))]
+        lanes = (pl.ds(0, 128), pl.ds(128, 128))
+        cols = (pl.ds(g * F, 128), pl.ds(g * F + 128, 128))
+
+        def all_to(n, pairs):
+            return [op for p, a in halves for op in to(a[n], functools.partial(pairs, p, a))]
+
         ops = [sems.copy(u_ref.at[1 - c, :, :, :, pl.ds(g * F, F)], v0.at[g], me.sibling())]
         yield
         wait(ops)
-
-        @pl.loop(0, 4)
-        def _(i):
+        for i in range(4):
             u0[g, i] = add([u_ref[c, i, :, :, pl.ds(g * F, F)], v0[g, i]]).astype(bf16)
-
-        ops = to("x", lambda d: (u0.at[g, me.step("x", d), :, :, left], v1.at[g, 0, d - 1]))
-        ops += to("z", lambda d: (u0.at[g, me.step("z", d), :, :, right], v1.at[g, 1, d - 1]))
-        yield
-        wait(ops)
-        w1[g, 0] = add([u0[g, x, :, :, left]] + [v1[g, 0, i] for i in range(3)]).astype(bf16)
-        w1[g, 1] = add([u0[g, z, :, :, right]] + [v1[g, 1, i] for i in range(3)]).astype(bf16)
-        ops = to("z", lambda d: (w1.at[g, 0, me.step("z", d)], v2.at[g, 0, d - 1]))
-        ops += to("x", lambda d: (w1.at[g, 1, me.step("x", d)], v2.at[g, 1, d - 1]))
-        yield
-        wait(ops)
-        v3[g, y, 0] = add([w1[g, 0, z]] + [v2[g, 0, i] for i in range(3)]).astype(bf16)
-        v3[g, y, 1] = add([w1[g, 1, x]] + [v2[g, 1, i] for i in range(3)]).astype(bf16)
-        ops = to("y", lambda d: (v3.at[g, y], v3.at[g, y]))
-        yield
-        wait(ops)
-        out_ref[c, x, z, :, one] = add([v3[g, i, 0] for i in range(4)]).astype(bf16)
-        out_ref[c, z, x, :, two] = add([v3[g, i, 1] for i in range(4)]).astype(bf16)
-        e, f = out_ref.at[c, x, z, :, one], out_ref.at[c, z, x, :, two]
-        ops = to("z", lambda d: (e, e)) + to("x", lambda d: (f, f))
-        yield
-        wait(ops)
-        h, i = out_ref.at[c, x, :, :, one], out_ref.at[c, z, :, :, two]
-        ops = to("x", lambda d: (h, h)) + to("z", lambda d: (i, i))
+        ops = all_to(0, lambda p, a, d: (u0.at[g, me.step(a[0], d), :, :, lanes[p]], v1.at[g, p, d - 1]))
+        yield
+        wait(ops)
+        for p, a in halves:
+            v2[g, p, me.at(a[1])] = add(
+                [u0[g, me.at(a[0]), :, :, lanes[p]]] + [v1[g, p, i] for i in range(3)]
+            ).astype(bf16)
+        ops = all_to(1, lambda p, a, d: (v2.at[g, p, me.at(a[1])], v2.at[g, p, me.at(a[1])]))
+        yield
+        wait(ops)
+        for p, a in halves:
+            v3[g, p, me.at(a[2])] = add([v2[g, p, i] for i in range(4)]).astype(bf16)
+        ops = all_to(2, lambda p, a, d: (v3.at[g, p, me.at(a[2])], v3.at[g, p, me.at(a[2])]))
+        yield
+        wait(ops)
+        for p, a in halves:
+            out_ref[c, me.at(a[0]), :, :, cols[p]] = add([v3[g, p, i] for i in range(4)]).astype(bf16)
+
+        def part(p, a):
+            return out_ref.at[c, me.at(a[0]), :, :, cols[p]]
+
+        ops = all_to(0, lambda p, a, d: (part(p, a), part(p, a)))
         yield
         wait(ops)
         k = out_ref.at[c, :, :, :, pl.ds(g * F, F)]
@@ -250,12 +251,14 @@
         yt = yt_ref[g, :, pl.ds(rb * RB, RB)]
         scale = s_ref[g] * (2.0 * LOG2E)
         m = None
-        for j in range(NK):
-            ks = pl.ds(j * KC, KC)
-            v = dot(words(g, j), yt) * scale - jnp.tile(bs[g % 2][ks, :], (1, RB // 128))
-            l[ks, :] = v
-            w = jnp.max(v.reshape(KC // 8, 8, RB), axis=0)
-            m = w if m is None else jnp.maximum(m, w)
+        for h in range(2):
+            big = dot(cb_ref[g, pl.ds(h * 2, 2)].reshape(K // 2, F), yt)
+            for j in range(NK // 2):
+                ks = pl.ds(h * K // 2 + j * KC, KC)
+                v = big[j * KC:(j + 1) * KC] * scale - jnp.tile(bs[g % 2][ks, :], (1, RB // 128))
+                l[ks, :] = v
+                w = jnp.max(v.reshape(KC // 8, 8, RB), axis=0)
+                m = w if m is None else jnp.maximum(m, w)
         return jnp.max(m, axis=0, keepdims=True)
 
     def softmax(l, m, p, cols):
@@ -282,10 +285,9 @@
         t = pq[:, :128]
         for i in range(1, R // 128):
             t = t + pq[:, i * 128:(i + 1) * 128]
-        ones = jnp.ones((8, 128), bf16)
-        row = lax.dot_general(ones, t, (((1,), (1,)), ((), ())), preferred_element_type=f32)
+        row = jnp.sum(t.astype(f32).T, axis=0, keepdims=True)
         for i in range(4):
-            n_ref[q, pl.ds(g * 4 + i, 1), :] = row[:1, i * 128:(i + 1) * 128]
+            n_ref[q, pl.ds(g * 4 + i, 1), :] = row[:, i * 128:(i + 1) * 128]
 
     def cross(g):
         cols = pl.ds(g * F, F)
@@ -329,87 +331,78 @@
     steps = [(g, rb) for g in range(G) for rb in range(NB)]
     m = logits(0, 0, l0)
     for t, (g, rb) in enumerate(steps):
-        if g + 1 < G:
-            if rb == 1:
-                wait(second[g + 1])
-                last.append(gather_core(g + 1))
-                if g + 2 < G:
-                    wait(first[g + 2])
-                    second.append(gather_second(g + 2))
-                if g + 3 < G:
-                    first.append(gather_first(g + 3))
-            if rb == 2:
-                wait(last[g + 1])
-                prepare(g + 1)
+        if g and rb % 2:
+            tick(t)
+        if g and rb == 1:
+            begin(t, cross_task(g - 1), (2, 4, 4, 4, 4, 2))
+        if g and rb == 3:
+            begin(t, sums_task(g - 1), (2, 4, 4))
+        if g + 1 < G and rb == 1:
+            wait(second[g + 1])
+            last.append(gather_core(g + 1))
+            if g + 2 < G:
+                wait(first[g + 2])
+                second.append(gather_second(g + 2))
+            if g + 3 < G:
+                first.append(gather_first(g + 3))
+        if g + 1 < G and rb == 3:
+            wait(last[g + 1])
+            prepare(g + 1)
         nm = logits(*steps[t + 1], ls[(t + 1) % 2]) if t + 1 < len(steps) else None
         softmax(ls[t % 2], m, ps[g % 2], pl.ds(rb * RB, RB))
         if t:
             pg, pr = steps[t - 1]
             recon(pg, pr, ps[pg % 2])
-        if g and g < G - 1:
-            sums(g - 1, rb, ps[(g - 1) % 2])
+        if g and rb < 2:
+            sums(g - 1, rb * 2, ps[(g - 1) % 2])
+            sums(g - 1, rb * 2 + 1, ps[(g - 1) % 2])
         if g and rb == 0:
             cross(g - 1)
-        tick(t)
-        if g and rb == 0:
-            begin(t, cross_task(g - 1), (1, 3, 2, 2, 2, 3, 1))
-        if g and g < G - 1 and rb == 3:
-            begin(t, sums_task(g - 1), (2, 4, 3))
         m = nm
 
     recon(G - 1, NB - 1, ps[(G - 1) % 2])
     cross(G - 1)
     late = 1 << 20
-    chain = cross_task(G - 1)
-    next(chain)
-    for q in range(NB):
-        sums(G - 2, q, ps[(G - 2) % 2])
-    one = sums_task(G - 2)
+    chain, two, count = cross_task(G - 1), sums_task(G - 1), counts_task()
+    one = tasks.pop()[0]
+
+    def others():
+        for entry in tasks:
+            entry[1] = 0
+        tick(late)
+
+    next(chain)
     next(one)
-    next(chain)
-    tick(late)
     for q in range(NB):
         sums(G - 1, q, ps[(G - 1) % 2])
-    two, count = sums_task(G - 1), counts_task()
     next(two)
     next(count)
+    next(chain)
+    next(two)
+    next(count)
+    others()
+    next(chain)
     next(one)
     next(count)
-    next(chain)
-    next(two)
-    for entry in tasks:
-        entry[1] = 0
-    tick(late)
-    next(count)
-    next(chain)
-    next(one)
-    for entry in tasks:
-        entry[1] = 0
-    tick(late)
-    next(count, None)
+    others()
     next(chain)
     next(two)
     next(one, None)
-    for entry in tasks:
-        entry[1] = 0
-    tick(late)
+    next(count, None)
+    others()
     next(chain)
     next(two, None)
     owner = owner_task()
     next(owner)
-    for entry in tasks:
-        entry[1] = 0
-    tick(late)
+    others()
     next(chain)
     while tasks:
-        for entry in tasks:
-            entry[1] = 0
-        tick(late)
+        others()
     next(owner, None)
     next(chain, None)
 
 
-COPIES = 3 + G * 13 + G * 13 + 10 + 6 + G * 29
+COPIES = 3 + G * 13 + G * 13 + 10 + 6 + G * 26
 
 
 def call(s, x, rot, own):
@@ -439,9 +432,8 @@
             pltpu.VMEM((3, 16, 128), f32), pltpu.VMEM((16, 128), f32), pltpu.VMEM((3, 16, 128), f32),
             pltpu.VMEM((16, 128), f32),
             pltpu.VMEM((G, 4, 4, 32, F), bf16), pltpu.VMEM((G, 4, 4, 32, F), bf16),
-            pltpu.VMEM((G, 2, 3, 4, 32, 128), bf16), pltpu.VMEM((G, 2, 4, 32, 128), bf16),
-            pltpu.VMEM((G, 2, 3, 32, 128), bf16), pltpu.VMEM((16, 128), bf16),
-            pltpu.VMEM((G, 4, 2, 32, 128), bf16),
+            pltpu.VMEM((G, 2, 3, 4, 32, 128), bf16), pltpu.VMEM((G, 2, 4, 4, 32, 128), bf16),
+            pltpu.VMEM((G, 2, 4, 4, 32, 128), bf16),
             pltpu.SemaphoreType.DMA((COPIES,)),
             pltpu.SemaphoreType.DMA((COPIES,)),
             pltpu.SemaphoreType.DMA((3,)),

time: 89.3 us -> 86.7 us (0.971)
  Pallas kernels: 88.3 us -> 85.7 us
    pallas_call x1, Pallas kernels: 85.6 us -> 83 us  [call(): pl.pallas_call(kernel, out_shape=[pltpu.VMEM((1, 64, F), f32), pltpu.VMEM...]
where the time goes in v4:
time: 86.7 us; the launch traced here: 86.6 us
  Pallas kernels  85.7 us (99%)
    pallas_call x1, Pallas kernels, call(): pl.pallas_call(kernel, out_shape=[pltpu.VMEM((1, 64, F), f32), pltpu.VMEM...  83 us
    pallas_call x1, Pallas kernels, finish(): pl.pallas_call(functools.partial(finish_kernel, scale), out_shape=[jax.Sh...  2.74 us

profile of v4, /device:TPU:1, one launch (start us, length us, event | category | flops | bytes accessed | tf_op | source)
XLA Modules:
  0.0 86.6 jit_solution(1085323305982808671)
XLA Ops:
  0.6 83.0 %quantizer_step.1 = (f32[1,64,256]{2,1,0:T(8,128)S(1)}, bf16[1024,1024]{1,0:T(8,128)(2,1)S(1)}, bf16[2,4,4,32,1024]{4,3,2,1,0:T(8,128)(2,1)S(1)}) custom-call(f32[4]{0:T(128)} %s_ref.1, bf16[1024,1024]{1,0:T(8,128)(2,1)} %x_hbm.1, bf16[1024,1024]{1,0:T(8,128)(2,1)} %rot_hbm.1, bf16[1,64,256]{2,1,0:T(8,128)(2,1)} %own_ref.1), custom_call_target="tpu_custom_call" | custom-call | tf_op jit(solution)/shard_map/quantizer_step/pallas_call | solution.py:410
  83.6 2.7 %write_results.1 = (f32[1,64,256]{2,1,0:T(8,128)}, bf16[1024,1024]{1,0:T(8,128)(2,1)}, f32[1024,1024]{1,0:T(8,128)}) custom-call(f32[1,64,256]{2,1,0:T(8,128)S(1)} %get-tuple-element.6.new_in, bf16[1024,1024]{1,0:T(8,128)(2,1)S(1)} %get-tuple-element.7.recon_in, bf16[1024,1024]{1,0:T(8,128)(2,1)S(1)} %bitcast.1), custom_call_target="tpu_custom_call" | custom-call | tf_op jit(solution)/shard_map/write_results/pallas_call | solution.py:466

commit v5 on v4

--- a/solution.py
+++ b/solution.py
@@ -125,14 +125,15 @@
         return [sems.copy(a, a, me.sibling())]
 
     def sums_task(g):
-        ops = [sems.copy(s_sum.at[g, :, :, 1 - c], r0.at[g], me.sibling())]
-        yield
-        wait(ops)
-
-        @pl.loop(0, 4)
-        def _(i):
-            s0[g, i] = add([s_sum[g, i, :, c], r0[g, i]]).astype(bf16)
-
+        ops = []
+        for h in range(2):
+            half = pl.ds(h * 2, 2)
+            ops.append(sems.copy(s_sum.at[g, half, :, 1 - c], r0.at[g, half], me.sibling()))
+            yield
+        for h in range(2):
+            wait([ops[h]])
+            for i in (h * 2, h * 2 + 1):
+                s0[g, i] = add([s_sum[g, i, :, c], r0[g, i]]).astype(bf16)
         ops = to("x", lambda d: (s0.at[g, me.step("x", d), :, TOP], r1.at[g, 0, d - 1]))
         ops += to("z", lambda d: (s0.at[g, :, me.step("z", d), LOW], r1.at[g, 1, d - 1]))
         yield
@@ -336,7 +337,9 @@
         if g and rb == 1:
             begin(t, cross_task(g - 1), (2, 4, 4, 4, 4, 2))
         if g and rb == 3:
-            begin(t, sums_task(g - 1), (2, 4, 4))
+            task = sums_task(g - 1)
+            next(task)
+            begin(t, task, (2, 4, 4))
         if g + 1 < G and rb == 1:
             wait(second[g + 1])
             last.append(gather_core(g + 1))
@@ -348,7 +351,6 @@
         if g + 1 < G and rb == 3:
             wait(last[g + 1])
             prepare(g + 1)
-        nm = logits(*steps[t + 1], ls[(t + 1) % 2]) if t + 1 < len(steps) else None
         softmax(ls[t % 2], m, ps[g % 2], pl.ds(rb * RB, RB))
         if t:
             pg, pr = steps[t - 1]
@@ -358,6 +360,7 @@
             sums(g - 1, rb * 2 + 1, ps[(g - 1) % 2])
         if g and rb == 0:
             cross(g - 1)
+        nm = logits(*steps[t + 1], ls[(t + 1) % 2]) if t + 1 < len(steps) else None
         m = nm
 
     recon(G - 1, NB - 1, ps[(G - 1) % 2])
@@ -375,7 +378,8 @@
     next(one)
     for q in range(NB):
         sums(G - 1, q, ps[(G - 1) % 2])
-    next(two)
+        if q % 2:
+            next(two)
     next(count)
     next(chain)
     next(two)
@@ -402,7 +406,7 @@
     next(chain, None)
 
 
-COPIES = 3 + G * 13 + G * 13 + 10 + 6 + G * 26
+COPIES = 3 + G * 13 + G * 14 + 10 + 6 + G * 26
 
 
 def call(s, x, rot, own):
@@ -450,8 +454,8 @@
     ]
     for op in moves:
         op.start()
-    n = D // 4
-    for i in range(4):
+    n = D // 8
+    for i in range(8):
         rows = pl.ds(i * n, n)
         buf[rows, :] = total_in[rows, :].astype(f32) * scale
         op = pltpu.make_async_copy(buf.at[rows, :], cross_out.at[rows, :], sem.at[2 + i])
@@ -472,7 +476,7 @@
         ],
         in_specs=[VM] * 3,
         out_specs=[any_place] * 3,
-        scratch_shapes=[pltpu.VMEM((D, D), f32), pltpu.SemaphoreType.DMA((6,))],
+        scratch_shapes=[pltpu.VMEM((D, D), f32), pltpu.SemaphoreType.DMA((10,))],
         compiler_params=pltpu.CompilerParams(vmem_limit_bytes=16 << 20),
         name="write_results",
     )(new, recon, total)

time: 86.7 us -> 83.7 us (0.965)
  Pallas kernels: 85.7 us -> 82.7 us
    pallas_call x1, Pallas kernels: 83 us -> 79.9 us  [call(): pl.pallas_call(kernel, out_shape=[pltpu.VMEM((1, 64, F), f32), pltpu.VMEM...]
where the time goes in v5:
time: 83.7 us; the launch traced here: 83.5 us
  Pallas kernels  82.7 us (99%)
    pallas_call x1, Pallas kernels, call(): pl.pallas_call(kernel, out_shape=[pltpu.VMEM((1, 64, F), f32), pltpu.VMEM...  79.9 us
    pallas_call x1, Pallas kernels, finish(): pl.pallas_call(functools.partial(finish_kernel, scale), out_shape=[jax.Sh...  2.76 us

profile of v5, /device:TPU:1, one launch (start us, length us, event | category | flops | bytes accessed | tf_op | source)
XLA Modules:
  0.0 83.5 jit_solution(17552821088082451658)
XLA Ops:
  0.6 79.9 %quantizer_step.1 = (f32[1,64,256]{2,1,0:T(8,128)S(1)}, bf16[1024,1024]{1,0:T(8,128)(2,1)S(1)}, bf16[2,4,4,32,1024]{4,3,2,1,0:T(8,128)(2,1)S(1)}) custom-call(f32[4]{0:T(128)} %s_ref.1, bf16[1024,1024]{1,0:T(8,128)(2,1)} %x_hbm.1, bf16[1024,1024]{1,0:T(8,128)(2,1)} %rot_hbm.1, bf16[1,64,256]{2,1,0:T(8,128)(2,1)} %own_ref.1), custom_call_target="tpu_custom_call" | custom-call | tf_op jit(solution)/shard_map/quantizer_step/pallas_call | solution.py:414
  80.6 2.8 %write_results.1 = (f32[1,64,256]{2,1,0:T(8,128)}, bf16[1024,1024]{1,0:T(8,128)(2,1)}, f32[1024,1024]{1,0:T(8,128)}) custom-call(f32[1,64,256]{2,1,0:T(8,128)S(1)} %get-tuple-element.6.new_in, bf16[1024,1024]{1,0:T(8,128)(2,1)S(1)} %get-tuple-element.7.recon_in, bf16[1024,1024]{1,0:T(8,128)(2,1)S(1)} %bitcast.1), custom_call_target="tpu_custom_call" | custom-call | tf_op jit(solution)/shard_map/write_results/pallas_call | solution.py:470

commit v6 on v5

--- a/solution.py
+++ b/solution.py
@@ -350,7 +350,6 @@
                 first.append(gather_first(g + 3))
         if g + 1 < G and rb == 3:
             wait(last[g + 1])
-            prepare(g + 1)
         softmax(ls[t % 2], m, ps[g % 2], pl.ds(rb * RB, RB))
         if t:
             pg, pr = steps[t - 1]
@@ -360,6 +359,8 @@
             sums(g - 1, rb * 2 + 1, ps[(g - 1) % 2])
         if g and rb == 0:
             cross(g - 1)
+        if g + 1 < G and rb == 3:
+            prepare(g + 1)
         nm = logits(*steps[t + 1], ls[(t + 1) % 2]) if t + 1 < len(steps) else None
         m = nm
 

time: 83.7 us -> 83.7 us (level)
  no operation moved by 1% of the time
where the time goes in v6:
time: 83.7 us; the launch traced here: 83.5 us
  Pallas kernels  82.7 us (99%)
    pallas_call x1, Pallas kernels, call(): pl.pallas_call(kernel, out_shape=[pltpu.VMEM((1, 64, F), f32), pltpu.VMEM...  79.9 us
    pallas_call x1, Pallas kernels, finish(): pl.pallas_call(functools.partial(finish_kernel, scale), out_shape=[jax.Sh...  2.76 us

profile of v6, /device:TPU:1, one launch (start us, length us, event | category | flops | bytes accessed | tf_op | source)
XLA Modules:
  0.0 83.5 jit_solution(12195249417394066077)
XLA Ops:
  0.6 79.9 %quantizer_step.1 = (f32[1,64,256]{2,1,0:T(8,128)S(1)}, bf16[1024,1024]{1,0:T(8,128)(2,1)S(1)}, bf16[2,4,4,32,1024]{4,3,2,1,0:T(8,128)(2,1)S(1)}) custom-call(f32[4]{0:T(128)} %s_ref.1, bf16[1024,1024]{1,0:T(8,128)(2,1)} %x_hbm.1, bf16[1024,1024]{1,0:T(8,128)(2,1)} %rot_hbm.1, bf16[1,64,256]{2,1,0:T(8,128)(2,1)} %own_ref.1), custom_call_target="tpu_custom_call" | custom-call | tf_op jit(solution)/shard_map/quantizer_step/pallas_call | solution.py:415
  80.6 2.8 %write_results.1 = (f32[1,64,256]{2,1,0:T(8,128)}, bf16[1024,1024]{1,0:T(8,128)(2,1)}, f32[1024,1024]{1,0:T(8,128)}) custom-call(f32[1,64,256]{2,1,0:T(8,128)S(1)} %get-tuple-element.6.new_in, bf16[1024,1024]{1,0:T(8,128)(2,1)S(1)} %get-tuple-element.7.recon_in, bf16[1024,1024]{1,0:T(8,128)(2,1)S(1)} %bitcast.1), custom_call_target="tpu_custom_call" | custom-call | tf_op jit(solution)/shard_map/write_results/pallas_call | solution.py:471
